TPU v7x, 32 devices: a whole 2x2x4 slice. The times are simulated.
32 devices in a mesh: seq: 4 (over y, x), dec: 8 (over z, core).
Axes of the slice: x: 2, y: 2, z: 4, core: 2. Of those that a mesh axis runs over, the one named last changes fastest.
Arguments:
- latents: bfloat16 [4, 4, 12, 8, 1024], P('seq', None, None, 'dec'), may hold values from -6 to 6
- cache_lat: bfloat16 [4, 4, 12, 8, 512], P('seq', None, None, 'dec'), may hold values from -6 to 6
- cache_act: bfloat16 [4, 4, 12, 8, 12288], P('seq', None, None, 'dec'), may hold values from -0.25 to 2
- w_in: bfloat16 [27, 16, 384], replicated, may hold values from -0.3125 to 0.3125
- w_mid: bfloat16 [27, 384, 384], replicated, may hold values from -0.0625 to 0.0625
- norm_gain: float32 [384], replicated, may hold values from 0.1 to 1.9
- clip_group: int32 [4, 4], replicated, may hold values from 0 to 3, as said below
- band_rows: int32 [4, 8], replicated, may hold values from 2 to 96, as said below
Outputs:
- decoded: bfloat16 [4, 8, 96, 4, 16, 384], P('seq', 'dec')
Inputs may be any that keep to these rules, and one draw needn't show every extreme that they name: For every sequence shard s, clip_group[s, :] names each of the 4 groups once. Each row of band_rows sums to 384; every band has 2 rows or more, and in each row one band has exactly 96 rows.
All inputs are finite; a program needn't handle non-finite values.
Results may differ from a plain program's by a relative error of at most 0.0029.
Values may be sent and summed in bfloat16 or wider, within the bound.
No kernel may reach another device: no remote copies, remote signals or barrier semaphores. Data moves between devices by JAX's collectives and lax.ppermute only.
A program may use at most 384 MiB of HBM per device.

v0:
```python
import jax
import jax.numpy as jnp
from jax import lax
from jax.sharding import PartitionSpec as P

F = 4
CT = 2
COLS = 16


EPSILON = 1e-06


def padded_2(cells, sides, width):
    for axis, dim in sides:
        count = lax.axis_size(axis)
        ends = count - 1
        head = lax.slice_in_dim(cells, 0, width, axis=dim)
        tail = lax.slice_in_dim(cells, cells.shape[dim] - width, cells.shape[dim], axis=dim)
        cells = jnp.concatenate(
            [
                lax.ppermute(tail, axis, [(i, (i + 1) % count) for i in range(ends)]),
                cells,
                lax.ppermute(head, axis, [((i + 1) % count, i) for i in range(ends)]),
            ],
            axis=dim,
        )
    return cells


def same_clip(rows_at, other_rows, height, stack_rows):
    inside = (other_rows >= 0) & (other_rows < stack_rows)
    return inside & (jnp.floor_divide(other_rows, height) == jnp.floor_divide(rows_at, height))


def assemble(own_rows, from_left, from_right, live_rows, margin):
    band_size = own_rows.shape[0]
    live_mask = jnp.arange(band_size, dtype=jnp.int32) < live_rows
    mask_shape = (band_size,) + (1,) * (own_rows.ndim - 1)
    kept_rows = jnp.where(live_mask.reshape(mask_shape), own_rows, jnp.zeros((), own_rows.dtype))
    extended = jnp.concatenate([from_left, kept_rows, jnp.zeros_like(from_right)], axis=0)
    zero_index = jnp.zeros((), jnp.int32)
    corner = (live_rows + margin,) + (zero_index,) * (own_rows.ndim - 1)
    return lax.dynamic_update_slice(extended, from_right, corner)


def banded_table(w_in):
    col_ids = jnp.arange(COLS, dtype=jnp.int32)
    shifts = jnp.stack(
        [
            (col_ids[:, None] == col_ids[None, :] + col_tap - 1).astype(jnp.float32)
            for col_tap in range(3)
        ]
    )
    taps = w_in.astype(jnp.float32).reshape(3, 3, 3, w_in.shape[1], w_in.shape[2])
    table = jnp.einsum("euv,abezc->abuzvc", shifts, taps)
    return table.reshape(9, COLS * w_in.shape[1], COLS * w_in.shape[2]).astype(jnp.bfloat16)


def conv_first(extended, first_row, table, height, stack_rows):
    out_rows = extended.shape[0] - 2
    frames = extended.shape[1] - CT
    width_in = extended.shape[2]
    width_out = table.shape[2]
    rows_at = first_row + 1 + jnp.arange(out_rows, dtype=jnp.int32)
    total_sum = jnp.zeros((out_rows, frames * width_out), jnp.float32)
    for row_tap in range(3):
        partial_sum = jnp.zeros((out_rows * frames, width_out), jnp.float32)
        for time_tap in range(3):
            slab = extended[row_tap : row_tap + out_rows, time_tap : time_tap + frames].reshape(
                out_rows * frames, width_in
            )
            partial_sum = partial_sum + jnp.dot(
                slab, table[time_tap * 3 + row_tap], preferred_element_type=jnp.float32
            )
        keep_mask = same_clip(rows_at, rows_at + row_tap - 1, height, stack_rows).astype(
            jnp.float32
        )[:, None]
        total_sum = total_sum + partial_sum.reshape(out_rows, frames * width_out) * keep_mask
    return total_sum.reshape(out_rows, frames, COLS, width_out // COLS)


def conv_second(act_big, first_row, w_mid, height, stack_rows):
    out_rows = act_big.shape[0] - 2
    frames = act_big.shape[1] - CT
    channels = act_big.shape[3]
    padded = jnp.pad(act_big, ((0, 0), (0, 0), (1, 1), (0, 0)))
    rows_at = first_row + 1 + jnp.arange(out_rows, dtype=jnp.int32)
    total_sum = jnp.zeros((out_rows, frames * COLS * w_mid.shape[2]), jnp.float32)
    for row_tap in range(3):
        partial_sum = jnp.zeros((out_rows * frames * COLS, w_mid.shape[2]), jnp.float32)
        for time_tap in range(3):
            for col_tap in range(3):
                tap_rows = padded[
                    row_tap : row_tap + out_rows,
                    time_tap : time_tap + frames,
                    col_tap : col_tap + COLS,
                    :,
                ].reshape(out_rows * frames * COLS, channels)
                partial_sum = partial_sum + jnp.dot(
                    tap_rows,
                    w_mid[time_tap * 9 + row_tap * 3 + col_tap],
                    preferred_element_type=jnp.float32,
                )
        keep_mask = same_clip(rows_at, rows_at + row_tap - 1, height, stack_rows).astype(
            jnp.float32
        )[:, None]
        total_sum = total_sum + partial_sum.reshape(out_rows, -1) * keep_mask
    return total_sum.reshape(out_rows, frames, COLS, w_mid.shape[2])


def activate(first_out, norm_gain):
    mean_square = jnp.mean(first_out * first_out, axis=-1, keepdims=True)
    return jax.nn.silu(first_out * lax.rsqrt(mean_square + EPSILON) * norm_gain).astype(
        jnp.bfloat16
    )


def band_slots(row_b, starts_b):
    owners = starts_b.shape[-1]
    band_of = jnp.sum(starts_b <= row_b[..., None], axis=-1) - 1
    safe_band = jnp.clip(band_of, 0, owners - 1)
    own_start = jnp.take_along_axis(starts_b, safe_band[..., None], axis=-1)[..., 0]
    entries = [(band_of, row_b - own_start + 2, jnp.ones(row_b.shape, bool))]
    return entries


def pack_rows(source_rows, entries, offset_b, slots, capacity, owners):
    flat_rows = source_rows.reshape(-1, source_rows.shape[-1])
    buffer_rows = jnp.zeros((slots, capacity, flat_rows.shape[-1]), flat_rows.dtype)
    for band, extended_at, valid in entries:
        target = jnp.where(valid, offset_b + band, slots).reshape(-1)
        slot_at = jnp.where(valid, extended_at // owners, 0).reshape(-1)
        buffer_rows = buffer_rows.at[target, slot_at].set(flat_rows, mode="drop")
    return buffer_rows


def shards(latents, cache_lat, cache_act, w_in, w_mid, norm_gain, clip_group, band_rows):
    groups = lax.axis_size("seq")
    owners = lax.axis_size("dec")
    seq_at = lax.axis_index("seq")
    dec_at = lax.axis_index("dec")
    per_owner = latents.shape[2]
    height = per_owner * owners
    stack_rows = groups * height
    band_max = 2 * stack_rows // owners
    capacity = (band_max + 4 + owners - 1) // owners
    table = banded_table(w_in)
    new_lat = latents.reshape(groups, per_owner, latents.shape[4])
    old_lat = cache_lat.reshape(groups, per_owner, cache_lat.shape[4])
    old_act = cache_act.reshape(groups, per_owner, cache_act.shape[4])
    starts = jnp.cumsum(band_rows, axis=1) - band_rows
    local_rows = jnp.arange(per_owner, dtype=jnp.int32)
    live_rows = band_rows[seq_at, dec_at]
    band_start = starts[seq_at, dec_at]
    ext_at = jnp.arange(band_max + 4, dtype=jnp.int32)
    ext_rows = band_start - 2 + ext_at
    ext_live = (ext_at < live_rows + 4) & (ext_rows >= 0) & (ext_rows < stack_rows)
    safe_rows = jnp.where(ext_live, ext_rows, 0)
    slot_back = ext_at // owners
    dest_group = clip_group[seq_at]
    row_at = seq_at * height + local_rows * owners + dec_at
    group_starts = starts[dest_group]
    row_b = jnp.broadcast_to(row_at[None, :], (groups, per_owner))
    starts_b = jnp.broadcast_to(group_starts[:, None, :], (groups, per_owner, owners))
    offset_b = jnp.broadcast_to((dest_group * owners)[:, None], (groups, per_owner))
    entries = band_slots(row_b, starts_b)
    slots = groups * owners
    arrived = (
        lax.all_to_all(
            pack_rows(new_lat, entries, offset_b, slots, capacity, owners),
            ("seq", "dec"),
            split_axis=0,
            concat_axis=0,
            tiled=True,
        ),
        lax.all_to_all(
            pack_rows(old_lat, entries, offset_b, slots, capacity, owners),
            ("seq", "dec"),
            split_axis=0,
            concat_axis=0,
            tiled=True,
        ),
        lax.all_to_all(
            pack_rows(old_act, entries, offset_b, slots, capacity, owners),
            ("seq", "dec"),
            split_axis=0,
            concat_axis=0,
            tiled=True,
        ),
    )
    source = jnp.floor_divide(safe_rows, height) * owners + safe_rows % owners

    def fetch(buffer_rows):
        picked = buffer_rows[source, slot_back]
        return jnp.where(ext_live[:, None], picked, jnp.zeros((), picked.dtype))

    ext_lat = fetch(arrived[0])
    ext_old = fetch(arrived[1])
    ext_cache = fetch(arrived[2])
    band_lat = ext_lat[2 : band_max + 2]
    band_old = ext_old[2 : band_max + 2]
    band_cache = ext_cache[2 : band_max + 2]
    layer_in = jnp.concatenate(
        [band_old.reshape(band_max, CT, -1), band_lat.reshape(band_max, F, -1)], axis=1
    )
    border_rows = jnp.stack(
        [layer_in[0], lax.dynamic_index_in_dim(layer_in, live_rows - 1, 0, keepdims=False)]
    )
    beside = padded_2(border_rows, (("dec", 0),), 1)
    extended = assemble(layer_in, beside[0:1], beside[3:4], live_rows, 1)
    first_out = conv_first(extended, band_start - 1, table, height, stack_rows)
    act_rows = jnp.concatenate(
        [band_cache.reshape(band_max, CT, COLS, -1), activate(first_out, norm_gain)], axis=1
    )
    act_border = jnp.stack(
        [act_rows[0], lax.dynamic_index_in_dim(act_rows, live_rows - 1, 0, keepdims=False)]
    )
    act_beside = padded_2(act_border, (("dec", 0),), 1)
    act_big = assemble(act_rows, act_beside[0:1], act_beside[3:4], live_rows, 1)
    live_mask = jnp.arange(band_max, dtype=jnp.int32) < live_rows
    second_out = conv_second(act_big, band_start - 1, w_mid, height, stack_rows)
    total_out = jnp.where(live_mask[:, None, None, None], first_out + second_out, 0.0).astype(
        jnp.bfloat16
    )
    return total_out.reshape((1, 1) + total_out.shape)


def solution(mesh):
    placed = (
        P("seq", None, None, "dec", None),
        P("seq", None, None, "dec", None),
        P("seq", None, None, "dec", None),
        P(),
        P(),
        P(),
        P(),
        P(),
    )
    return jax.shard_map(
        shards,
        mesh=mesh,
        in_specs=placed,
        out_specs=P("seq", "dec", None, None, None, None),
        check_vma=False,
    )
```

profile of v0, /device:TPU:11, one launch (start us, length us, event | category | flops | bytes accessed | tf_op | source)
XLA Modules:
  0.0 841.0 jit_solution(12888276533220508603)
XLA Ops:
  22.9 7.6 all-to-all-done
  42.6 33.5 %scatter_fusion.2 = bf16[32,13,12288]{2,0,1:T(8,128)(2,1)} fusion(bf16[32,13,12288]{2,0,1:T(8,128)(2,1)} %broadcast_in_dim.169, s32[48]{0:T(128)S(1)} %fusion.124, bf16[48,12288]{1,0:T(8,128)(2,1)S(1)} %reshape.928), kind=kCustom, calls=%fused_computation.7 | custom fusion | bytes 3539328 | tf_op jit(solution)/shard_map/scatter | solution.py:134
  76.0 13.2 %copy.47 = bf16[32,13,12288]{2,1,0:T(8,128)(2,1)} copy(bf16[32,13,12288]{2,0,1:T(8,128)(2,1)} %scatter_fusion.2) | data formatting | bytes 20447232 | tf_op jit(solution)/shard_map/scatter | solution.py:134
  101.2 12.8 %convert_bitcast_fusion = bf16[3,3,16,16,16,384]{5,4,3,1,0,2:T(8,128)(2,1)} fusion(bf16[3,3,3,16,384]{4,3,2,1,0:T(8,128)(2,1)S(1)} %bitcast.344, pred[1,16,16]{2,0,1:T(4,128)(4,1)S(1)} %get-tuple-element.51, pred[1,16,16]{2,0,1:T(4,128)(4,1)S(1)} %get-tuple-element.52, pred[1,16,16]{2,0,1:T(4,128)(4,1)S(1)} %iota_compare_fusion.2), kind=kOutput, calls=%fused_computation.8 | convolution fusion | flops 99091968 | bytes 28644096 | tf_op jit(solution)/shard_map/euv,abezc->abuzvc/dot_general | solution.py:56
  114.0 19.5 %copy.45 = bf16[3,3,16,16,16,384]{5,4,3,2,1,0:T(8,128)(2,1)} copy(bf16[3,3,16,16,16,384]{5,4,3,1,0,2:T(8,128)(2,1)} %convert_bitcast_fusion) | data formatting | bytes 56623104 | tf_op jit(solution)/shard_map/convert_element_type | solution.py:57
  133.5 39.8 %convert_element_type.79 = bf16[9,256,6144]{2,1,0:T(8,128)(2,1)} reshape(bf16[3,3,16,16,16,384]{5,4,3,2,1,0:T(8,128)(2,1)} %copy.45) | data formatting | bytes 56623104 | tf_op jit(solution)/shard_map/convert_element_type | solution.py:57
  187.5 178.4 %collective-permute-done = bf16[1,6,256]{2,1,0:T(8,128)(2,1)S(1)} collective-permute-done((bf16[1,6,256]{2,1,0:T(8,128)(2,1)S(1)}, bf16[1,6,256]{2,1,0:T(8,128)(2,1)S(1)}, u32[]{:S(2)}, u32[]{:S(2)}) %collective-permute-start) | collective-permute-done | bytes 3104 | tf_op jit(solution)/shard_map/ppermute | solution.py:22
  374.7 7.3 add_add_fusion.5
  382.1 9.2 %copy.52 = f32[48,8,16,384]{3,2,1,0:T(8,128)} copy(f32[48,8,16,384]{3,1,2,0:T(8,128)} %bitcast.264) | data formatting | bytes 18874368
  398.0 7.2 add_add_fusion.4
  405.2 9.6 %copy.53 = f32[48,8,16,384]{3,2,1,0:T(8,128)} copy(f32[48,8,16,384]{3,1,2,0:T(8,128)} %bitcast.265) | data formatting | bytes 18874368
  428.8 13.9 %add_add_fusion.3 = f32[384,6144]{1,0:T(8,128)} fusion(f32[384,6144]{1,0:T(8,128)} %fusion.3, f32[384,6144]{1,0:T(8,128)} %fusion.2, bf16[384,256]{1,0:T(8,128)(2,1)S(1)} %reshape.844, bf16[9,256,6144]{2,1,0:T(8,128)(2,1)} %convert_element_type.79), kind=kOutput, calls=%fused_computation.37 | convolution fusion | flops 1212678144 | bytes 31653888 | tf_op jit(solution)/shard_map/dot_general | solution.py:73
  442.7 9.7 %copy.54 = f32[48,8,16,384]{3,2,1,0:T(8,128)} copy(f32[48,8,16,384]{3,1,2,0:T(8,128)} %bitcast.263) | data formatting | bytes 18874368
  452.5 9.8 %multiply_reduce_fusion = (f32[96,4,16]{2,1,0:T(4,128)S(1)}, f32[96,4,16,384]{3,2,1,0:T(8,128)}) fusion(f32[96,4,16,384]{3,2,1,0:T(8,128)} %bitcast.258, f32[96]{0:T(128)S(1)} %get-tuple-element.49, f32[96,4,16,384]{3,2,1,0:T(8,128)S(1)} %bitcast.257, f32[96]{0:T(128)S(1)} %copy-done.10, f32[96,4,16,384]{3,2,1,0:T(8,128)S(1)} %bitcast.253, ...), kind=kLoop, calls=%fused_computation.35 | loop fusion | flops 16508928 | bytes 37774464 | tf_op jit(solution)/shard_map/reduce_sum | solution.py:113
  462.7 7.9 multiply_convert_fusion
  470.5 13.3 %copy.48 = bf16[32,13,12288]{2,0,1:T(8,128)(2,1)} copy(bf16[32,13,12288]{2,1,0:T(8,128)(2,1)} %all-to-all-done.2) | data formatting | bytes 20447232 | tf_op jit(solution)/shard_map/all_to_all | solution.py:184
  483.8 9.0 %gather_fusion.3 = bf16[100,12288]{1,0:T(8,128)(2,1)S(1)} fusion(bf16[32,13,12288]{2,0,1:T(8,128)(2,1)} %copy.48, s32[100]{0:T(128)S(1)} %fusion.118), kind=kCustom, calls=%fused_computation.3 | custom fusion | bytes 4916000 | tf_op jit(solution)/shard_map/gather | solution.py:195
  506.2 60.9 %pad_slice_fusion.12 = (bf16[96,4,16,384]{3,2,1,0:T(8,128)(2,1)}, bf16[96,4,16,384]{3,2,1,0:T(8,128)(2,1)}, bf16[96,4,16,384]{3,2,1,0:T(8,128)(2,1)}, bf16[96,4,...) fusion(bf16[98,6,16,384]{3,2,1,0:T(8,128)(2,1)} %constant_dynam, ...), kind=kLoop, calls=%fused_computation.21 | loop fusion | bytes 106315776 | tf_op jit(solution)/shard_map/slice | solution.py:94
  567.2 26.4 %fusion.126 = (bf16[96,4,16,384]{3,2,1,0:T(8,128)(2,1)}, bf16[96,4,16,384]{3,2,1,0:T(8,128)(2,1)}, bf16[96,4,16,384]{3,2,1,0:T(8,128)(2,1)}, bf16[96,4,16,384]{3...) fusion(bf16[98,6,16,384]{3,2,1,0:T(8,128)(2,1)} %constant_dynam, ...), kind=kLoop, calls=%fused_computation.234 | loop fusion | bytes 78004224 | tf_op jit(solution)/shard_map/slice | solution.py:94
  593.6 9.3 %fusion.59 = f32[6144,384]{1,0:T(8,128)} fusion(bf16[6144,384]{1,0:T(8,128)(2,1)} %bitcast.313, bf16[27,384,384]{2,1,0:T(8,128)(2,1)} %param.12), kind=kOutput, calls=%fused_computation.112 | convolution fusion | flops 1811939328 | bytes 14450688 | tf_op jit(solution)/shard_map/dot_general | solution.py:100
  728.4 30.1 %add_add_fusion.2 = f32[6144,384]{1,0:T(8,128)} fusion(f32[6144,384]{1,0:T(8,128)} %fusion.57, f32[6144,384]{1,0:T(8,128)} %fusion.59, f32[6144,384]{1,0:T(8,128)} %fusion.61, f32[6144,384]{1,0:T(8,128)} %fusion.63, f32[6144,384]{1,0:T(8,128)} %fusion.65, f32[6144,384]{1,0:T(8,128)} %fusion.67, f32[6144,384]{1,0:T(8,128)} %fusion.71, ...), kind=kOutput, calls=%fused_computation.33 | convolution fusion | flops 1830813696 | bytes 89948160 | tf_op jit(solution)/shard_map/dot_general | solution.py:100
  758.5 29.9 %add_add_fusion.1 = f32[6144,384]{1,0:T(8,128)} fusion(f32[6144,384]{1,0:T(8,128)} %fusion.37, f32[6144,384]{1,0:T(8,128)} %fusion.39, f32[6144,384]{1,0:T(8,128)} %fusion.41, f32[6144,384]{1,0:T(8,128)} %fusion.43, f32[6144,384]{1,0:T(8,128)} %fusion.45, f32[6144,384]{1,0:T(8,128)} %fusion.47, f32[6144,384]{1,0:T(8,128)} %fusion.51, ...), kind=kOutput, calls=%fused_computation.32 | convolution fusion | flops 1830813696 | bytes 89948160 | tf_op jit(solution)/shard_map/dot_general | solution.py:100
  788.4 29.8 %add_add_fusion = f32[6144,384]{1,0:T(8,128)} fusion(f32[6144,384]{1,0:T(8,128)} %fusion.17, f32[6144,384]{1,0:T(8,128)} %fusion.19, f32[6144,384]{1,0:T(8,128)} %fusion.21, f32[6144,384]{1,0:T(8,128)} %fusion.23, f32[6144,384]{1,0:T(8,128)} %fusion.25, f32[6144,384]{1,0:T(8,128)} %fusion.27, f32[6144,384]{1,0:T(8,128)} %fusion.31, ...), kind=kOutput, calls=%fused_computation.31 | convolution fusion | flops 1830813696 | bytes 89948160 | tf_op jit(solution)/shard_map/dot_general | solution.py:100
  818.2 22.3 %select_convert_fusion = bf16[1,1,96,4,16,384]{5,4,3,2,1,0:T(8,128)(2,1)} fusion(f32[1,1,96,4,16,384]{5,4,3,2,1,0:T(8,128)} %bitcast.262, f32[1,1,96,4,16,384]{5,4,3,2,1,0:T(8,128)} %bitcast.261, f32[1,1,96,4,16,384]{5,4,3,2,1,0:T(8,128)} %bitcast.260, f32[1,1,96,4,16,384]{5,4,3,2,1,0:T(8,128)} %bitcast.259, f32[1,1,96,4,16,384]{5,4,3,2,1,0:T(8,128)} %bitcast.254, ...), kind=kLoop, calls=%fused_computation.30 | loop fusion | flops 30670848 | bytes 61342944 | tf_op jit(solution)/shard_map/convert_element_type | solution.py:223
  (278 shorter events, 225.6 us)
Async XLA Ops:
  0.0 36.4 %copy-start.1 = (bf16[1,4,12,1,12288]{4,1,3,2,0:T(4,128)(2,1)S(1)}, bf16[1,4,12,1,12288]{4,1,3,2,0:T(4,128)(2,1)}, u32[]{:S(2)}) copy-start(bf16[1,4,12,1,12288]{4,1,3,2,0:T(4,128)(2,1)} %param.10) | copy-start | bytes 3538948
  10.5 20.1 %all-to-all-start = ((bf16[32,13,512]{2,1,0:T(8,128)(2,1)}), bf16[32,13,512]{2,1,0:T(8,128)(2,1)S(1)}, u32[]{:S(2)}, u32[]{:S(2)}) async-start(bf16[32,13,512]{2,1,0:T(8,128)(2,1)} %copy.39), calls=%async_computation | async-start | bytes 1048576 | tf_op jit(solution)/shard_map/all_to_all | solution.py:177
  30.6 58.7 %all-to-all-start.1 = ((bf16[32,13,1024]{2,1,0:T(8,128)(2,1)}), bf16[32,13,1024]{2,1,0:T(8,128)(2,1)}, u32[]{:S(2)}, u32[]{:S(2)}) async-start(bf16[32,13,1024]{2,1,0:T(8,128)(2,1)} %copy.42), calls=%async_computation.1 | async-start | bytes 2097152 | tf_op jit(solution)/shard_map/all_to_all | solution.py:170
  89.3 11.9 %copy-start.2 = (bf16[27,16,384]{2,1,0:T(8,128)(2,1)S(1)}, bf16[27,16,384]{2,1,0:T(8,128)(2,1)}, u32[]{:S(2)}) copy-start(bf16[27,16,384]{2,1,0:T(8,128)(2,1)} %param.11) | copy-start | bytes 995332
  89.3 381.3 %all-to-all-start.2 = ((bf16[32,13,12288]{2,1,0:T(8,128)(2,1)}), bf16[32,13,12288]{2,1,0:T(8,128)(2,1)}, u32[]{:S(2)}, u32[]{:S(2)}) async-start(bf16[32,13,12288]{2,1,0:T(8,128)(2,1)} %copy.47), calls=%async_computation.2 | async-start | bytes 25165824 | tf_op jit(solution)/shard_map/all_to_all | solution.py:184
  173.9 324.4 %copy-start.3 = (pred[96]{0:T(512)(128)(4,1)}, pred[96]{0:T(512)(128)(4,1)S(1)}, u32[]{:S(2)}) copy-start(pred[96]{0:T(512)(128)(4,1)S(1)} %iota_compare_fusion.3) | copy-start | bytes 292
  174.6 277.9 %copy-start.6 = (f32[96]{0:T(128)}, f32[96]{0:T(128)S(1)}, u32[]{:S(2)}) copy-start(f32[96]{0:T(128)S(1)} %and_convert_fusion.2) | copy-start | bytes 1156
  175.8 276.6 %copy-start.8 = (f32[96]{0:T(128)}, f32[96]{0:T(128)S(1)}, u32[]{:S(2)}) copy-start(f32[96]{0:T(128)S(1)} %get-tuple-element.49) | copy-start | bytes 1156
  181.7 184.2 %collective-permute-start = (bf16[1,6,256]{2,1,0:T(8,128)(2,1)S(1)}, bf16[1,6,256]{2,1,0:T(8,128)(2,1)S(1)}, u32[]{:S(2)}, u32[]{:S(2)}) collective-permute-start(bf16[1,6,256]{2,1,0:T(8,128)(2,1)S(1)} %get-tuple-element.46), channel_id=1, source_target_pairs={{0,1},{1,2},{2,3},{3,4},{4,5},{5,6},{6,7},{8,9},{9,10},{10,11},{11... | collective-permute-start | bytes 9224 | tf_op jit(solution)/shard_map/ppermute | solution.py:22
  185.3 182.2 %collective-permute-start.1 = (bf16[1,6,256]{2,1,0:T(8,128)(2,1)S(1)}, bf16[1,6,256]{2,1,0:T(8,128)(2,1)S(1)}, u32[]{:S(2)}, u32[]{:S(2)}) collective-permute-start(bf16[1,6,256]{2,1,0:T(8,128)(2,1)S(1)} %get-tuple-element.45), channel_id=1, source_target_pairs={{1,0},{2,1},{3,2},{4,3},{5,4},{6,5},{7,6},{9,8},{10,9},{11,10},{12... | collective-permute-start | bytes 9224 | tf_op jit(solution)/shard_map/ppermute | solution.py:24
  428.8 23.7 %slice-start = ((s8[9437184]{0:T(1024)(128)(4,1)}), s8[4194304]{0:T(1024)(128)(4,1)S(1)}, s32[]{:S(2)}) async-start(s8[9437184]{0:T(1024)(128)(4,1)} %bitcast.251), calls=%async_computation.3 | async-start | bytes 8388608
  428.8 23.7 %slice-start.1 = ((s8[9437184]{0:T(1024)(128)(4,1)}), s8[4194304]{0:T(1024)(128)(4,1)S(1)}, s32[]{:S(2)}) async-start(s8[9437184]{0:T(1024)(128)(4,1)} %bitcast.251), calls=%async_computation.4 | async-start | bytes 8388608
  428.8 23.7 %slice-start.3 = ((s8[9437184]{0:T(1024)(128)(4,1)}), s8[4194304]{0:T(1024)(128)(4,1)S(1)}, s32[]{:S(2)}) async-start(s8[9437184]{0:T(1024)(128)(4,1)} %bitcast.255), calls=%async_computation.6 | async-start | bytes 8388608
  428.8 23.7 %slice-start.4 = ((s8[9437184]{0:T(1024)(128)(4,1)}), s8[4194304]{0:T(1024)(128)(4,1)S(1)}, s32[]{:S(2)}) async-start(s8[9437184]{0:T(1024)(128)(4,1)} %bitcast.255), calls=%async_computation.7 | async-start | bytes 8388608
  442.7 9.8 %slice-start.5 = ((s8[9437184]{0:T(1024)(128)(4,1)}), s8[1048576]{0:T(1024)(128)(4,1)S(1)}, s32[]{:S(2)}) async-start(s8[9437184]{0:T(1024)(128)(4,1)} %bitcast.255), calls=%async_computation.8 | async-start | bytes 2097152
  442.7 9.8 %copy-start.10 = (f32[96]{0:T(128)S(1)}, f32[96]{0:T(128)}, u32[]{:S(2)}) copy-start(f32[96]{0:T(128)} %get-tuple-element.50) | copy-start | bytes 1156
  452.5 10.1 %copy-start.5 = (f32[384]{0:T(512)S(1)}, f32[384]{0:T(512)}, u32[]{:S(2)}) copy-start(f32[384]{0:T(512)} %param.13) | copy-start | bytes 4612
  495.2 6.4 collective-permute-start.2
  499.7 5.9 collective-permute-start.3
  593.6 15.7 %slice-start.52 = ((s8[7962624]{0:T(1024)(128)(4,1)}), s8[4194304]{0:T(1024)(128)(4,1)S(1)}, s32[]{:S(2)}) async-start(s8[7962624]{0:T(1024)(128)(4,1)} %bitcast.342), calls=%async_computation.55 | async-start | bytes 8388608
  788.3 29.8 %copy-start.4 = (pred[96]{0:T(512)(128)(4,1)S(1)}, pred[96]{0:T(512)(128)(4,1)}, u32[]{:S(2)}) copy-start(pred[96]{0:T(512)(128)(4,1)} %copy-done.3) | copy-start | bytes 292
  788.3 29.9 %copy-start.7 = (f32[96]{0:T(128)S(1)}, f32[96]{0:T(128)}, u32[]{:S(2)}) copy-start(f32[96]{0:T(128)} %copy-done.6) | copy-start | bytes 1156
  788.4 29.9 %copy-start.9 = (f32[96]{0:T(128)S(1)}, f32[96]{0:T(128)}, u32[]{:S(2)}) copy-start(f32[96]{0:T(128)} %copy-done.8) | copy-start | bytes 1156
  788.4 29.9 %copy-start.11 = (f32[96]{0:T(128)S(1)}, f32[96]{0:T(128)}, u32[]{:S(2)}) copy-start(f32[96]{0:T(128)} %get-tuple-element.50) | copy-start | bytes 1156
  (49 other events, 277.5 us)
where the time goes:
time: 851 us; the launch traced here: 841 us
  matrix products  292 us (34%)
  local copies, waits for them, and re-layouts  274 us (32%)
  waiting for transfers between devices  188 us (22%)
  other arithmetic  52.9 us (6%)
  starting transfers between devices  29.2 us (3%)
    dot_general x27, matrix products, conv_second(): jnp.dot(tap_rows, w_mid[time_tap * 9 + row_tap * 3 + col_tap], preferred_...  224 us
    ppermute x2, waiting for transfers between devices, padded_2(): lax.ppermute(tail, axis, [(i, (i + 1) % count) for i in range(ends)])  178 us
    slice x2, local copies, waits for them, and re-layouts, conv_second(): padded[row_tap:row_tap + out_rows, time_tap:time_tap + frames, col_tap:co...  87.4 us
    convert_element_type x2, local copies, waits for them, and re-layouts, banded_table(): table.reshape(9, COLS * w_in.shape[1], COLS * w_in.shape[2])  59.2 us
    scatter x6, local copies, waits for them, and re-layouts, pack_rows(): buffer_rows = buffer_rows.at[target, slot_at].set(flat_rows, mode='drop')  55.9 us
    dot_general x9, matrix products, conv_first(): jnp.dot(slab, table[time_tap * 3 + row_tap], preferred_element_type=jnp.f...  55.4 us
    unnamed x141, local copies, waits for them, and re-layouts  32.5 us
    convert_element_type x1, other arithmetic, shards(): jnp.where(live_mask[:, None, None, None], first_out + second_out, 0.0)  22.3 us
  transfers between devices with their start and end apart: 7, of which 3 were waited for; matrix products, arithmetic and copies ran while one was open for 30% of the time, Pallas kernels for 0%

commit v1 on v0

v1 whole, which is shorter than its diff:
```python
import functools

import jax
import jax.numpy as jnp
from jax import lax
from jax.experimental import pallas as pl
from jax.experimental.pallas import tpu as pltpu
from jax.sharding import PartitionSpec as P

F = 4
CT = 2
COLS = 16
LANES = 128
EPSILON = 1e-06
VMEM = 56 * 1024 * 1024
F32 = jnp.float32
BF16 = jnp.bfloat16


def ceil_to(value, unit):
    return (value + unit - 1) // unit * unit


def band_start(bands, group, owner, owners):
    total = jnp.int32(0)
    for other in range(owners):
        total = total + jnp.where(other < owner, bands[group, other], 0)
    return total


def first_unit(start, margin, source, owners, units, capacity):
    unit = (start - margin - source + owners - 1 + 2 * owners) // owners - 2
    return jnp.clip(unit, 0, units - capacity)


def clip_of(groups_ref, shard, group, clips):
    found = jnp.int32(0)
    for clip in range(clips):
        found = found + jnp.where(groups_ref[shard, clip] == group, clip, 0)
    return found


def pack_latents(groups_ref, lat_ref, old_ref, out_ref, scratch, *, per_owner, clips, rows):
    shard = lax.axis_index("seq")
    for row in range(per_owner):
        for frame in range(CT + F):
            for half in range(2):
                if frame < CT:
                    tile = frame * 2 + half
                    value = old_ref[row, :, tile * LANES : (tile + 1) * LANES]
                else:
                    tile = (frame - CT) * 2 + half
                    value = lat_ref[row, :, tile * LANES : (tile + 1) * LANES]
                at = row * 12 + half * (CT + F) + frame
                scratch[pl.ds(at, clips, stride=rows), :] = value.astype(F32)
    for group in range(clips):
        clip = clip_of(groups_ref, shard, group, clips)
        out_ref[group] = scratch[pl.ds(pl.multiple_of(clip * rows, 8), rows), :].astype(BF16)


def pack_caches(groups_ref, act_ref, out_ref, scratch, *, per_step, clips):
    shard = lax.axis_index("seq")
    tiles = act_ref.shape[2] // LANES
    depth = tiles // (CT * COLS)
    for row in range(per_step):
        for frame in range(CT):
            for col in range(COLS):
                for part in range(depth):
                    tile = (frame * COLS + col) * depth + part
                    at = row * tiles + (frame * depth + part) * COLS + col
                    value = act_ref[row, :, tile * LANES : (tile + 1) * LANES]
                    scratch[pl.ds(at, clips, stride=per_step * tiles), :] = value.astype(F32)
    for group in range(clips):
        clip = clip_of(groups_ref, shard, group, clips)
        size = per_step * tiles
        out_ref[group] = scratch[pl.ds(pl.multiple_of(clip * size, 8), size), :].astype(BF16)


def slice_latents(bands, in_ref, out_ref, scratch, *, owners, units, capacity, per_owner):
    group = lax.axis_index("seq")
    source = lax.axis_index("dec")
    rows = out_ref.shape[1]
    for shard in range(in_ref.shape[0]):
        size = per_owner * 12
        scratch[pl.ds(shard * size, in_ref.shape[1]), :] = in_ref[shard].astype(F32)
    for owner in range(owners):
        start = band_start(bands, group, owner, owners)
        unit = first_unit(start, 2, source, owners, units, capacity)
        out_ref[owner] = scratch[pl.ds(unit * 12, rows), :].astype(BF16)


def slice_caches(bands, in_ref, out_ref, sems, *, owners, units, capacity, tiles):
    group = lax.axis_index("seq")
    source = lax.axis_index("dec")
    copies = []
    for owner in range(owners):
        start = band_start(bands, group, owner, owners)
        unit = first_unit(start, 1, source, owners, units, capacity)
        copy = pltpu.make_async_copy(
            in_ref.at[pl.ds(pl.multiple_of(unit * tiles, 16), capacity * tiles)],
            out_ref.at[owner],
            sems.at[owner],
        )
        copy.start()
        copies.append(copy)
    for copy in copies:
        copy.wait()


def shift_columns(sums, width):
    rows = sums.shape[0]
    col = lax.rem(lax.broadcasted_iota(jnp.int32, (rows, width), 0), COLS)
    left = pltpu.roll(sums[:, :width], 1, 0)
    right = pltpu.roll(sums[:, 2 * width :], rows - 1, 0)
    total = sums[:, width : 2 * width] + jnp.where(col > 0, left, 0.0)
    return total + jnp.where(col < COLS - 1, right, 0.0)


def weight_copies(mid_ref, weights, sems, channels, time_taps):
    copies = []
    for tap in range(time_taps * 9):
        copies.append(
            pltpu.make_async_copy(
                mid_ref.at[tap],
                weights.at[
                    pl.ds(tap // 3 * channels, channels), pl.ds(tap % 3 * channels, channels)
                ],
                sems.at[tap],
            )
        )
    return copies


def new_frames(
    bands, lat_ref, win_ref, gain_ref, mid_ref, out_ref, part_ref,
    weights, table, xs, windows, first, act, sems,
    *, owners, units, capacity, height, block, band_max, channels,
):
    group = lax.axis_index("seq")
    owner = lax.axis_index("dec")
    live = bands[group, owner]
    start = band_start(bands, group, owner, owners)
    step = pl.program_id(0)
    ext = band_max + 4
    depth = channels // LANES
    zero_row = ext
    edge = lax.rem(height - lax.rem(start - 1 + height, height), height)

    @pl.when(step == 0)
    def _():
        copies = weight_copies(mid_ref, weights, sems, channels, 3)
        for copy in copies:
            copy.start()
        table[...] = jnp.zeros(table.shape, BF16)
        for tap in range(9):
            for col in range(4):
                for shift in range(3):
                    table[
                        pl.ds(tap * LANES + (col + shift + 1) * 16, 16),
                        pl.ds(col * channels, channels),
                    ] = win_ref[tap * 3 + shift]
        per_source = lat_ref.shape[1]
        for source in range(owners):
            xs[pl.ds(source * per_source, per_source), :] = lat_ref[source].astype(F32)
        lane = lax.broadcasted_iota(jnp.int32, (8, LANES), 1)

        def fill(row, carry):
            at = jnp.clip(start - 2 + row, 0, units * owners - 1)
            source = lax.rem(at, owners)
            unit = first_unit(start, 2, source, owners, units, capacity)
            slot = jnp.clip(at // owners - unit, 0, capacity - 1)
            base = source * per_source + slot * 12
            for tap in range(3):
                left = xs[pl.ds(base + tap, 8), :]
                right = xs[pl.ds(base + tap + CT + F, 8), :]
                left_up, left_down = pltpu.roll(left, 32, 1), pltpu.roll(left, 96, 1)
                right_up, right_down = pltpu.roll(right, 32, 1), pltpu.roll(right, 96, 1)
                into = pl.ds(row * F, 8)
                windows[0, tap, into, :] = jnp.where(lane < 32, 0.0, left_up)
                windows[1, tap, into, :] = jnp.where(lane < 96, left_down, right_down)
                windows[2, tap, into, :] = jnp.where(lane < 32, left_up, right_up)
                windows[3, tap, into, :] = jnp.where(lane < 96, right_down, 0.0)
            return carry

        lax.fori_loop(0, ext, fill, 0)
        for tap in range(3):
            for quarter in range(4):
                windows[quarter, tap, pl.ds(ext * F, 16), :] = jnp.zeros((16, LANES), F32)

        rows = ext * F
        at_row = lax.broadcasted_iota(jnp.int32, (rows, LANES), 0) // F
        above = ((at_row != edge) & (at_row != edge + height)).astype(F32)
        below = ((at_row != edge - 1) & (at_row != edge - 1 + height)).astype(F32)

        def convolve(quarter, carry):
            pieces = []
            for tap in range(3):
                for row_tap in range(3):
                    piece = windows[quarter, tap, pl.ds(row_tap * F, rows), :]
                    if row_tap == 0:
                        piece = piece * above
                    if row_tap == 2:
                        piece = piece * below
                    pieces.append(piece.astype(BF16))
            slab = jnp.concatenate(pieces, axis=1)
            for col in range(4):
                sums = jnp.dot(
                    slab, table[:, pl.ds(col * channels, channels)], preferred_element_type=F32
                )
                for part in range(depth):
                    first[part, pl.ds(quarter * 4 + col, rows, stride=COLS), :] = sums[
                        :, part * LANES : (part + 1) * LANES
                    ]
            return carry

        lax.fori_loop(0, 4, convolve, 0)
        gain = gain_ref[...]

        def activate(row, carry):
            into = pl.ds(pl.multiple_of(row * F * COLS, F * COLS), F * COLS)
            value = jnp.concatenate([first[part, into, :] for part in range(depth)], axis=1)
            mean_square = jnp.mean(value * value, axis=-1, keepdims=True)
            value = value * lax.rsqrt(mean_square + EPSILON) * gain
            value = value / (1.0 + jnp.exp(-value))
            act[row] = value.astype(BF16).reshape(F, COLS, channels)
            return carry

        lax.fori_loop(0, live + 2, activate, 0)
        act[zero_row] = jnp.zeros((F, COLS, channels), BF16)
        for copy in copies:
            copy.wait()

    begin = step * block

    @pl.when(begin < live)
    def _():
        source_rows = [[], [], []]
        for row in range(block):
            at = jnp.minimum(begin + row, live - 1) + 1
            is_first = (at == edge) | (at == edge + height)
            is_last = (at == edge - 1) | (at == edge - 1 + height)
            source_rows[0].append(jnp.where(is_first, zero_row, at - 1))
            source_rows[1].append(at)
            source_rows[2].append(jnp.where(is_last, zero_row, at + 1))

        def slab(frames):
            pieces = []
            for frame, count in frames:
                for row_tap in range(3):
                    parts = [
                        act[at, frame : frame + count].reshape(count * COLS, channels)
                        for at in source_rows[row_tap]
                    ]
                    pieces.append(jnp.concatenate(parts, axis=0))
            return jnp.concatenate(pieces, axis=1)

        def finish(frames, weight_from, frame_from, count):
            sums = jnp.dot(slab(frames), weights[weight_from:, :], preferred_element_type=F32)
            total = shift_columns(sums, channels)
            parts = []
            for row in range(block):
                at = (begin + row + 1) * F * COLS + frame_from * COLS
                into = pl.ds(pl.multiple_of(at, COLS), count * COLS)
                parts.append(
                    jnp.concatenate([first[part, into, :] for part in range(depth)], axis=1)
                )
            return total + jnp.concatenate(parts, axis=0)

        taps = 3 * channels
        late = finish([(0, 2), (1, 2), (2, 2)], 0, 2, 2)
        at_row = lax.broadcasted_iota(jnp.int32, late.shape, 0) // (2 * COLS)
        late = jnp.where(at_row < live - begin, late, 0.0)
        out_ref[...] = late.astype(BF16).reshape(block, 2, COLS, channels)
        part_ref[:, 1] = finish([(0, 1), (1, 1)], taps, 1, 1).reshape(block, COLS, channels)
        part_ref[:, 0] = finish([(0, 1)], 2 * taps, 0, 1).reshape(block, COLS, channels)

    @pl.when(begin >= live)
    def _():
        out_ref[...] = jnp.zeros(out_ref.shape, BF16)


def cached_frames(
    bands, cache_ref, part_ref, mid_ref, late_ref, out_ref, weights, cache, sems, cache_sem,
    *, owners, units, capacity, height, block, channels,
):
    del late_ref
    group = lax.axis_index("seq")
    owner = lax.axis_index("dec")
    live = bands[group, owner]
    start = band_start(bands, group, owner, owners)
    step = pl.program_id(0)
    depth = channels // LANES
    slots = owners * capacity
    edge = lax.rem(height - lax.rem(start - 1 + height, height), height)

    @pl.when(step == 0)
    def _():
        copies = weight_copies(mid_ref, weights, sems, channels, 2)
        load = pltpu.make_async_copy(cache_ref, cache.at[pl.ds(0, slots)], cache_sem)
        load.start()
        for copy in copies:
            copy.start()
        cache[slots] = jnp.zeros(cache.shape[1:], BF16)
        load.wait()
        for copy in copies:
            copy.wait()

    begin = step * block

    @pl.when(begin < live)
    def _():
        def slot_of(at):
            row = jnp.clip(start - 1 + at, 0, units * owners - 1)
            source = lax.rem(row, owners)
            unit = first_unit(start, 1, source, owners, units, capacity)
            return source * capacity + jnp.clip(row // owners - unit, 0, capacity - 1)

        source_rows = [[], [], []]
        for row in range(block):
            at = jnp.minimum(begin + row, live - 1) + 1
            is_first = (at == edge) | (at == edge + height)
            is_last = (at == edge - 1) | (at == edge - 1 + height)
            source_rows[0].append(jnp.where(is_first, slots, slot_of(at - 1)))
            source_rows[1].append(slot_of(at))
            source_rows[2].append(jnp.where(is_last, slots, slot_of(at + 1)))

        def slab(frames):
            pieces = []
            for frame in frames:
                for row_tap in range(3):
                    for part in range(depth):
                        from_tile = (frame * depth + part) * COLS
                        parts = [
                            cache[at, from_tile : from_tile + COLS, :]
                            for at in source_rows[row_tap]
                        ]
                        pieces.append(jnp.concatenate(parts, axis=0))
            return jnp.concatenate(pieces, axis=1)

        at_row = lax.broadcasted_iota(jnp.int32, (block * COLS, channels), 0) // COLS
        taps = 3 * channels
        for frame, frames in ((0, (0, 1)), (1, (1,))):
            sums = jnp.dot(
                slab(frames), weights[: len(frames) * taps, :], preferred_element_type=F32
            )
            total = shift_columns(sums, channels) + part_ref[:, frame].reshape(
                block * COLS, channels
            )
            total = jnp.where(at_row < live - begin, total, 0.0)
            out_ref[:, frame] = total.astype(BF16).reshape(block, COLS, channels)

    @pl.when(begin >= live)
    def _():
        out_ref[...] = jnp.zeros(out_ref.shape, BF16)


def params(**extra):
    return pltpu.CompilerParams(vmem_limit_bytes=VMEM, **extra)


def shards(latents, cache_lat, cache_act, w_in, w_mid, norm_gain, clip_group, band_rows):
    groups = lax.axis_size("seq")
    owners = lax.axis_size("dec")
    clips = latents.shape[1]
    per_owner = latents.shape[2]
    channels = w_mid.shape[2]
    units = groups * per_owner
    height = per_owner * owners
    stack_rows = groups * height
    band_max = 2 * stack_rows // owners
    lat_capacity = (band_max + 4 + owners - 1) // owners
    act_capacity = (band_max + 2 + owners - 1) // owners
    block = 8
    any_space = pl.BlockSpec(memory_space=pl.ANY)
    in_vmem = pl.BlockSpec(memory_space=pltpu.VMEM)

    def rows_first(array):
        return jnp.transpose(array[0, :, :, 0, :], (1, 0, 2))

    lat, old, act = rows_first(latents), rows_first(cache_lat), rows_first(cache_act)
    tiles = act.shape[2] // LANES
    lat_rows = ceil_to(per_owner * 12, 16)
    packed_lat = pl.pallas_call(
        functools.partial(pack_latents, per_owner=per_owner, clips=clips, rows=lat_rows),
        grid_spec=pltpu.PrefetchScalarGridSpec(
            num_scalar_prefetch=1,
            grid=(),
            in_specs=[in_vmem, in_vmem],
            out_specs=in_vmem,
            scratch_shapes=[pltpu.VMEM((clips * lat_rows, LANES), F32)],
        ),
        out_shape=jax.ShapeDtypeStruct((clips, lat_rows, LANES), BF16),
        compiler_params=params(),
        name="pack_latents",
    )(clip_group, lat, old)
    per_step = 3
    packed_act = pl.pallas_call(
        functools.partial(pack_caches, per_step=per_step, clips=clips),
        grid_spec=pltpu.PrefetchScalarGridSpec(
            num_scalar_prefetch=1,
            grid=(per_owner // per_step,),
            in_specs=[
                pl.BlockSpec((per_step, clips, act.shape[2]), lambda step, _: (step, 0, 0))
            ],
            out_specs=pl.BlockSpec(
                (clips, per_step * tiles, LANES), lambda step, _: (0, step, 0)
            ),
            scratch_shapes=[pltpu.VMEM((clips * per_step * tiles, LANES), F32)],
        ),
        out_shape=jax.ShapeDtypeStruct((clips, per_owner * tiles, LANES), BF16),
        compiler_params=params(),
        name="pack_caches",
    )(clip_group, act)

    def exchange(array, axis):
        return lax.all_to_all(array, axis, split_axis=0, concat_axis=0, tiled=True)

    group_lat = exchange(packed_lat, "seq")
    group_act = exchange(packed_act, "seq")
    slice_rows = ceil_to(lat_capacity * 12, 16)
    band_lat = pl.pallas_call(
        functools.partial(
            slice_latents, owners=owners, units=units, capacity=lat_capacity, per_owner=per_owner
        ),
        grid_spec=pltpu.PrefetchScalarGridSpec(
            num_scalar_prefetch=1,
            grid=(),
            in_specs=[in_vmem],
            out_specs=in_vmem,
            scratch_shapes=[pltpu.VMEM((units * 12 + lat_rows + slice_rows, LANES), F32)],
        ),
        out_shape=jax.ShapeDtypeStruct((owners, slice_rows, LANES), BF16),
        compiler_params=params(),
        name="slice_latents",
    )(band_rows, group_lat)
    band_lat = exchange(band_lat, "dec")
    band_act = pl.pallas_call(
        functools.partial(
            slice_caches, owners=owners, units=units, capacity=act_capacity, tiles=tiles
        ),
        grid_spec=pltpu.PrefetchScalarGridSpec(
            num_scalar_prefetch=1,
            grid=(),
            in_specs=[any_space],
            out_specs=any_space,
            scratch_shapes=[pltpu.SemaphoreType.DMA((owners,))],
        ),
        out_shape=jax.ShapeDtypeStruct((owners, act_capacity * tiles, LANES), BF16),
        compiler_params=params(),
        name="slice_caches",
    )(band_rows, group_act.reshape(units * tiles, LANES))
    band_lat, band_act = lax.optimization_barrier((band_lat, band_act))
    band_act = exchange(band_act, "dec")

    ext = band_max + 4
    late, part = pl.pallas_call(
        functools.partial(
            new_frames, owners=owners, units=units, capacity=lat_capacity, height=height,
            block=block, band_max=band_max, channels=channels,
        ),
        grid_spec=pltpu.PrefetchScalarGridSpec(
            num_scalar_prefetch=1,
            grid=(band_max // block,),
            in_specs=[in_vmem, in_vmem, in_vmem, any_space],
            out_specs=[
                pl.BlockSpec((block, 2, COLS, channels), lambda step, _: (step, 1, 0, 0)),
                pl.BlockSpec((block, 2, COLS, channels), lambda step, _: (step, 0, 0, 0)),
            ],
            scratch_shapes=[
                pltpu.VMEM((9 * channels, 3 * channels), BF16),
                pltpu.VMEM((9 * LANES, 4 * channels), BF16),
                pltpu.VMEM((owners * slice_rows + 16, LANES), F32),
                pltpu.VMEM((4, 3, ext * F + 16, LANES), F32),
                pltpu.VMEM((channels // LANES, (ext + block) * F * COLS, LANES), F32),
                pltpu.VMEM((ext + 1, F, COLS, channels), BF16),
                pltpu.SemaphoreType.DMA((27,)),
            ],
        ),
        out_shape=[
            jax.ShapeDtypeStruct((band_max, F, COLS, channels), BF16),
            jax.ShapeDtypeStruct((band_max, 2, COLS, channels), F32),
        ],
        compiler_params=params(dimension_semantics=("arbitrary",)),
        cost_estimate=pl.CostEstimate(
            flops=2 * band_max * 9 * COLS * 9 * channels * channels,
            bytes_accessed=16 * 1024 * 1024,
            transcendentals=0,
        ),
        name="new_frames",
    )(band_rows, band_lat, w_in, norm_gain.reshape(1, channels), w_mid)

    slots = owners * act_capacity
    decoded = pl.pallas_call(
        functools.partial(
            cached_frames, owners=owners, units=units, capacity=act_capacity, height=height,
            block=block, channels=channels,
        ),
        grid_spec=pltpu.PrefetchScalarGridSpec(
            num_scalar_prefetch=1,
            grid=(band_max // block,),
            in_specs=[
                any_space,
                pl.BlockSpec((block, 2, COLS, channels), lambda step, _: (step, 0, 0, 0)),
                any_space,
                any_space,
            ],
            out_specs=pl.BlockSpec(
                (block, 2, COLS, channels), lambda step, _: (step, 0, 0, 0)
            ),
            scratch_shapes=[
                pltpu.VMEM((6 * channels, 3 * channels), BF16),
                pltpu.VMEM((slots + 1, tiles, LANES), BF16),
                pltpu.SemaphoreType.DMA((18,)),
                pltpu.SemaphoreType.DMA,
            ],
        ),
        out_shape=jax.ShapeDtypeStruct((band_max, F, COLS, channels), BF16),
        input_output_aliases={4: 0},
        compiler_params=params(dimension_semantics=("arbitrary",)),
        cost_estimate=pl.CostEstimate(
            flops=2 * band_max * 3 * COLS * 9 * channels * channels,
            bytes_accessed=16 * 1024 * 1024,
            transcendentals=0,
        ),
        name="cached_frames",
    )(band_rows, band_act.reshape(slots, tiles, LANES), part, w_mid, late)
    return decoded.reshape((1, 1) + decoded.shape)


def solution(mesh):
    placed = (
        P("seq", None, None, "dec", None),
        P("seq", None, None, "dec", None),
        P("seq", None, None, "dec", None),
        P(),
        P(),
        P(),
        P(),
        P(),
    )
    return jax.shard_map(
        shards,
        mesh=mesh,
        in_specs=placed,
        out_specs=P("seq", "dec", None, None, None, None),
        check_vma=False,
    )
```

time: 851 us -> 234 us (0.27)
  the two profiles are of different devices: /device:TPU:11 before, /device:TPU:3 now
where the time goes in v1:
time: 234 us; the launch traced here: 233 us
  Pallas kernels  200 us (85%)
  starting transfers between devices  19.7 us (8%)
  waiting for transfers between devices  10.8 us (5%)
    pallas_call x1, Pallas kernels, shards(): pl.pallas_call(functools.partial(new_frames, owners=owners, units=units,...  85.6 us
    pallas_call x1, Pallas kernels, shards(): pl.pallas_call(functools.partial(slice_caches, owners=owners, units=units...  79.3 us
    pallas_call x1, Pallas kernels, shards(): pl.pallas_call(functools.partial(cached_frames, owners=owners, units=unit...  25.9 us
    all_to_all x4, starting transfers between devices, exchange(): return lax.all_to_all(array, axis, split_axis=0, concat_axis=0, tiled=True)  19.7 us
    all_to_all x4, waiting for transfers between devices, exchange(): return lax.all_to_all(array, axis, split_axis=0, concat_axis=0, tiled=True)  10.8 us
    pallas_call x1, Pallas kernels, shards(): pl.pallas_call(functools.partial(pack_caches, per_step=per_step, clips=cl...  4.86 us
  transfers between devices with their start and end apart: 4, of which 1 were waited for; matrix products, arithmetic and copies ran while one was open for 0% of the time, Pallas kernels for 74%

profile of v1, /device:TPU:3, one launch (start us, length us, event | category | flops | bytes accessed | tf_op | source)
XLA Modules:
  0.0 233.1 jit_solution(4988820625079618666)
XLA Ops:
  0.0 2.4 %pack_latents.1 = bf16[4,144,128]{2,1,0:T(8,128)(2,1)} custom-call(s32[4,4]{1,0:T(4,128)} %groups_ref.3, bf16[12,4,1024]{2,1,0:T(4,128)(2,1)} %bitcast.15, bf16[12,4,512]{2,1,0:T(4,128)(2,1)} %bitcast.16), custom_call_target="tpu_custom_call" | custom-call | tf_op jit(solution)/shard_map/pack_latents/pallas_call | solution.py:383
  2.4 3.7 %all-to-all-start = ((bf16[4,144,128]{2,1,0:T(8,128)(2,1)}), bf16[4,144,128]{2,1,0:T(8,128)(2,1)S(1)}, u32[]{:S(2)}, u32[]{:S(2)}) async-start(bf16[4,144,128]{2,1,0:T(8,128)(2,1)} %pack_latents.1), calls=%async_computation | async-start | bytes 294912 | tf_op jit(solution)/shard_map/all_to_all | solution.py:416
  6.1 4.9 %pack_caches.1 = bf16[4,1152,128]{2,1,0:T(8,128)(2,1)} custom-call(s32[4,4]{1,0:T(4,128)} %groups_ref.3, bf16[12,4,12288]{2,1,0:T(4,128)(2,1)} %bitcast.14), custom_call_target="tpu_custom_call" | custom-call | tf_op jit(solution)/shard_map/pack_caches/pallas_call | solution.py:397
  10.9 0.0 all-to-all-done.in_ref
  10.9 0.0 copy-start.2
  10.9 3.6 %all-to-all-start.2 = ((bf16[4,1152,128]{2,1,0:T(8,128)(2,1)}), bf16[4,1152,128]{2,1,0:T(8,128)(2,1)S(1)}, u32[]{:S(2)}, u32[]{:S(2)}) async-start(bf16[4,1152,128]{2,1,0:T(8,128)(2,1)} %pack_caches.1), calls=%async_computation.2 | async-start | bytes 2359296 | tf_op jit(solution)/shard_map/all_to_all | solution.py:416
  14.6 0.0 copy-done.2
  14.6 2.4 %slice_latents.1 = bf16[8,160,128]{2,1,0:T(8,128)(2,1)} custom-call(s32[4,8]{1,0:T(4,128)} %bands.7, bf16[4,144,128]{2,1,0:T(8,128)(2,1)} %copy-done.2), custom_call_target="tpu_custom_call" | custom-call | tf_op jit(solution)/shard_map/slice_latents/pallas_call | solution.py:421
  16.9 10.8 %all-to-all-done.2 = bf16[4,1152,128]{2,1,0:T(8,128)(2,1)S(1)} async-done(((bf16[4,1152,128]{2,1,0:T(8,128)(2,1)}), bf16[4,1152,128]{2,1,0:T(8,128)(2,1)S(1)}, u32[]{:S(2)}, u32[]{:S(2)}) %all-to-all-start.2) | async-done | bytes 1179680 | tf_op jit(solution)/shard_map/all_to_all | solution.py:416
  27.8 7.3 %all-to-all-start.1 = ((bf16[8,160,128]{2,1,0:T(8,128)(2,1)}), bf16[8,160,128]{2,1,0:T(8,128)(2,1)S(1)}, u32[]{:S(2)}, u32[]{:S(2)}) async-start(bf16[8,160,128]{2,1,0:T(8,128)(2,1)} %slice_latents.1), calls=%async_computation.1 | async-start | bytes 655360 | tf_op jit(solution)/shard_map/all_to_all | solution.py:416
  35.1 0.0 copy-done
  35.1 79.3 %slice_caches.1 = bf16[8,1248,128]{2,1,0:T(8,128)(2,1)} custom-call(s32[4,8]{1,0:T(4,128)} %bands.7, bf16[4608,128]{1,0:T(8,128)(2,1)} %bitcast.12), custom_call_target="tpu_custom_call" | custom-call | tf_op jit(solution)/shard_map/slice_caches/pallas_call | solution.py:437
  114.4 0.0 copy-start.4
  114.4 0.0 all-to-all-done.1.lat_ref
  114.4 0.0 copy-start.3
  114.4 5.1 %all-to-all-start.3 = ((bf16[8,1248,128]{2,1,0:T(8,128)(2,1)}), bf16[8,1248,128]{2,1,0:T(8,128)(2,1)S(1)}, u32[]{:S(2)}, u32[]{:S(2)}) async-start(bf16[8,1248,128]{2,1,0:T(8,128)(2,1)} %slice_caches.1), calls=%async_computation.3 | async-start | bytes 5111808 | tf_op jit(solution)/shard_map/all_to_all | solution.py:416
  119.6 0.0 copy-done.4
  119.6 0.5 reshape.14.gain_ref
  120.1 0.0 copy-done.3
  120.1 85.6 %new_frames.1 = (bf16[96,4,16,384]{3,2,1,0:T(8,128)(2,1)}, f32[96,2,16,384]{3,2,1,0:T(8,128)}) custom-call(s32[4,8]{1,0:T(4,128)} %bands.7, bf16[8,160,128]{2,1,0:T(8,128)(2,1)} %copy-done.3, bf16[27,16,384]{2,1,0:T(8,128)(2,1)} %win_ref.1, f32[1,384]{1,0:T(1,128)} %reshape.14.gain_ref, bf16[27,384,384]{2,1,0:T(8,128)(2,1)} %mid_ref.3), custom_call_target="tpu_custom_call" | custom-call | flops 36691771392 | bytes 16777216 | tf_op jit(solution)/shard_map/new_frames/pallas_call | solution.py:456
  205.7 0.0 all-to-all-done.3
  205.7 0.0 copy-start.1
  205.7 1.5 copy-done.1
  207.2 25.9 %cached_frames.1 = bf16[96,4,16,384]{3,2,1,0:T(8,128)(2,1)} custom-call(s32[4,8]{1,0:T(4,128)} %bands.7, bf16[104,96,128]{2,1,0:T(8,128)(2,1)} %bitcast.13, f32[96,2,16,384]{3,2,1,0:T(8,128)} %get-tuple-element.11.part_ref, bf16[27,384,384]{2,1,0:T(8,128)(2,1)} %mid_ref.3, ...), custom_call_target="tpu_custom_call", output_to_operand_aliasing={{}: (4, {})} | custom-call | flops 12230590464 | bytes 16777216 | tf_op jit(solution)/shard_map/cached_frames/pallas_call | solution.py:493
  (1 shorter events, 0.0 us)
Async XLA Ops:
  2.4 8.5 %all-to-all-start = ((bf16[4,144,128]{2,1,0:T(8,128)(2,1)}), bf16[4,144,128]{2,1,0:T(8,128)(2,1)S(1)}, u32[]{:S(2)}, u32[]{:S(2)}) async-start(bf16[4,144,128]{2,1,0:T(8,128)(2,1)} %pack_latents.1), calls=%async_computation | async-start | bytes 294912 | tf_op jit(solution)/shard_map/all_to_all | solution.py:416
  10.9 3.6 %copy-start.2 = (bf16[4,144,128]{2,1,0:T(8,128)(2,1)}, bf16[4,144,128]{2,1,0:T(8,128)(2,1)S(1)}, u32[]{:S(2)}) copy-start(bf16[4,144,128]{2,1,0:T(8,128)(2,1)S(1)} %all-to-all-done.in_ref) | copy-start | bytes 442372
  10.9 16.9 %all-to-all-start.2 = ((bf16[4,1152,128]{2,1,0:T(8,128)(2,1)}), bf16[4,1152,128]{2,1,0:T(8,128)(2,1)S(1)}, u32[]{:S(2)}, u32[]{:S(2)}) async-start(bf16[4,1152,128]{2,1,0:T(8,128)(2,1)} %pack_caches.1), calls=%async_computation.2 | async-start | bytes 2359296 | tf_op jit(solution)/shard_map/all_to_all | solution.py:416
  27.8 7.3 %copy-start = (bf16[4,1152,128]{2,1,0:T(8,128)(2,1)}, bf16[4,1152,128]{2,1,0:T(8,128)(2,1)S(1)}, u32[]{:S(2)}) copy-start(bf16[4,1152,128]{2,1,0:T(8,128)(2,1)S(1)} %all-to-all-done.2) | copy-start | bytes 3538948
  27.8 86.6 %all-to-all-start.1 = ((bf16[8,160,128]{2,1,0:T(8,128)(2,1)}), bf16[8,160,128]{2,1,0:T(8,128)(2,1)S(1)}, u32[]{:S(2)}, u32[]{:S(2)}) async-start(bf16[8,160,128]{2,1,0:T(8,128)(2,1)} %slice_latents.1), calls=%async_computation.1 | async-start | bytes 655360 | tf_op jit(solution)/shard_map/all_to_all | solution.py:416
  114.4 5.1 %copy-start.4 = (f32[384]{0:T(512)S(1)}, f32[384]{0:T(512)}, u32[]{:S(2)}) copy-start(f32[384]{0:T(512)} %param.13) | copy-start | bytes 4612
  114.4 5.7 %copy-start.3 = (bf16[8,160,128]{2,1,0:T(8,128)(2,1)}, bf16[8,160,128]{2,1,0:T(8,128)(2,1)S(1)}, u32[]{:S(2)}) copy-start(bf16[8,160,128]{2,1,0:T(8,128)(2,1)S(1)} %all-to-all-done.1.lat_ref) | copy-start | bytes 983044
  114.4 91.2 %all-to-all-start.3 = ((bf16[8,1248,128]{2,1,0:T(8,128)(2,1)}), bf16[8,1248,128]{2,1,0:T(8,128)(2,1)S(1)}, u32[]{:S(2)}, u32[]{:S(2)}) async-start(bf16[8,1248,128]{2,1,0:T(8,128)(2,1)} %slice_caches.1), calls=%async_computation.3 | async-start | bytes 5111808 | tf_op jit(solution)/shard_map/all_to_all | solution.py:416
  205.7 1.5 copy-start.1

commit v2 on v1

v2 whole, which is shorter than its diff:
```python
import functools

import jax
import jax.numpy as jnp
from jax import lax
from jax.experimental import pallas as pl
from jax.experimental.pallas import tpu as pltpu
from jax.sharding import PartitionSpec as P

F = 4
CT = 2
COLS = 16
LANES = 128
EPSILON = 1e-06
F32 = jnp.float32
BF16 = jnp.bfloat16


def band_start(bands, group, owner, owners):
    total = jnp.int32(0)
    for other in range(owners):
        total = total + jnp.where(other < owner, bands[group, other], 0)
    return total


def first_unit(start, margin, source, owners, units, capacity):
    unit = (start - margin - source + owners - 1 + 2 * owners) // owners - 2
    return jnp.clip(unit, 0, units - capacity)


def clip_of(groups_ref, shard, group, clips):
    found = jnp.int32(0)
    for clip in range(clips):
        found = found + jnp.where(groups_ref[shard, clip] == group, clip, 0)
    return found


def pack_latents(groups_ref, lat_ref, old_ref, *refs, per_owner, clips):
    *outs, scratch = refs
    shard = lax.axis_index("seq")
    rows = outs[0].shape[0]
    for row in range(per_owner):
        for frame in range(CT + F):
            for half in range(2):
                if frame < CT:
                    tile = frame * 2 + half
                    value = old_ref[row, :, tile * LANES : (tile + 1) * LANES]
                else:
                    tile = (frame - CT) * 2 + half
                    value = lat_ref[row, :, tile * LANES : (tile + 1) * LANES]
                at = row * 12 + half * (CT + F) + frame
                scratch[pl.ds(at, clips, stride=rows), :] = value.astype(F32)
    for other in range(clips):
        clip = clip_of(groups_ref, shard, shard ^ other, clips)
        outs[other][...] = scratch[pl.ds(pl.multiple_of(clip * rows, 8), rows), :].astype(BF16)


def pack_caches(groups_ref, act_ref, *refs, per_step, clips):
    *outs, scratch = refs
    shard = lax.axis_index("seq")
    tiles = act_ref.shape[2] // LANES
    depth = tiles // (CT * COLS)
    size = per_step * tiles
    for row in range(per_step):
        for frame in range(CT):
            for col in range(COLS):
                for part in range(depth):
                    tile = (frame * COLS + col) * depth + part
                    at = row * tiles + (frame * depth + part) * COLS + col
                    value = act_ref[row, :, tile * LANES : (tile + 1) * LANES]
                    scratch[pl.ds(at, clips, stride=size), :] = value.astype(F32)
    for other in range(clips):
        clip = clip_of(groups_ref, shard, shard ^ other, clips)
        outs[other][...] = scratch[pl.ds(pl.multiple_of(clip * size, 8), size), :].astype(BF16)


def slice_latents(bands, *refs, owners, units, capacity, per_owner):
    *ins, out_ref, scratch = refs
    group = lax.axis_index("seq")
    source = lax.axis_index("dec")
    rows = out_ref.shape[1]
    size = per_owner * 12
    for other, in_ref in enumerate(ins):
        scratch[pl.ds((group ^ other) * size, size), :] = in_ref[:size, :].astype(F32)
    value = pltpu.roll(scratch[: units * 12, :], 64, 1)
    lane = lax.broadcasted_iota(jnp.int32, value.shape, 1)
    for width in (32, 16):
        up, down = pltpu.roll(value, width, 1), pltpu.roll(value, LANES - width, 1)
        value = jnp.where(lane & width == 0, down, up)
    scratch[: units * 12, :] = value
    for owner in range(owners):
        start = band_start(bands, group, owner, owners)
        unit = first_unit(start, 2, source, owners, units, capacity)
        out_ref[owner] = scratch[pl.ds(unit * 12, rows), :].astype(BF16)


def slice_caches(bands, *refs, owners, units, capacity, tiles):
    *ins, out_ref, scratch, in_sems, sems = refs
    group = lax.axis_index("seq")
    source = lax.axis_index("dec")
    size = ins[0].shape[0]
    copies = []
    for other, in_ref in enumerate(ins):
        into = pl.ds(pl.multiple_of((group ^ other) * size, 16), size)
        copies.append(pltpu.make_async_copy(in_ref, scratch.at[into], in_sems.at[other]))
    for copy in copies:
        copy.start()
    for copy in copies:
        copy.wait()
    copies = []
    for owner in range(owners):
        start = band_start(bands, group, owner, owners)
        unit = first_unit(start, 1, source, owners, units, capacity)
        copies.append(
            pltpu.make_async_copy(
                scratch.at[pl.ds(pl.multiple_of(unit * tiles, 16), capacity * tiles)],
                out_ref.at[owner],
                sems.at[owner],
            )
        )
    for copy in copies:
        copy.start()
    for copy in copies:
        copy.wait()


def shift_columns(sums, width):
    rows = sums.shape[0]
    col = lax.rem(lax.broadcasted_iota(jnp.int32, (rows, width), 0), COLS)
    left = pltpu.roll(sums[:, :width], 1, 0)
    right = pltpu.roll(sums[:, 2 * width :], rows - 1, 0)
    total = sums[:, width : 2 * width] + jnp.where(col > 0, left, 0.0)
    return total + jnp.where(col < COLS - 1, right, 0.0)


def weight_copies(mid_ref, weights, sems, channels):
    copies = []
    for tap in range(27):
        into = weights.at[
            pl.ds(tap // 3 * channels, channels), pl.ds(tap % 3 * channels, channels)
        ]
        copies.append(pltpu.make_async_copy(mid_ref.at[tap], into, sems.at[tap]))
    return copies


def new_frames(
    bands, lat_ref, win_ref, gain_ref, mid_ref, out_ref, part_ref, early_ref,
    weights, table, xs, windows, first, act, sems, out_sem,
    *, owners, units, capacity, height, block, band_max, channels,
):
    group = lax.axis_index("seq")
    owner = lax.axis_index("dec")
    live = bands[group, owner]
    start = band_start(bands, group, owner, owners)
    step = pl.program_id(0)
    ext = band_max + 4
    zero_row = ext
    edge = lax.rem(height - lax.rem(start - 1 + height, height), height)
    early = pltpu.make_async_copy(weights.at[pl.ds(0, 6 * channels)], early_ref, out_sem)

    def clip_edges(at):
        is_first = (at == edge) | (at == edge + height)
        is_last = (at == edge - 1) | (at == edge - 1 + height)
        return is_first, is_last

    @pl.when(step == 0)
    def _():
        copies = weight_copies(mid_ref, weights, sems, channels)
        for copy in copies:
            copy.start()
        table[...] = jnp.zeros(table.shape, BF16)
        for time_tap in range(3):
            for row_tap in range(3):
                for col_tap in range(3):
                    into = row_tap * 2 * LANES + (0, 64, LANES)[time_tap]
                    into += ((0, 112, 96), (0, -16, -32), (0, 112, 96))[time_tap][col_tap]
                    table[pl.ds(into, 16), :] = win_ref[time_tap * 9 + row_tap * 3 + col_tap]
        per_source = lat_ref.shape[1]
        for source in range(owners):
            value = lat_ref[source].astype(F32)
            xs[0, pl.ds(source * per_source, per_source), :] = value
            xs[1, pl.ds(source * per_source, per_source), :] = pltpu.roll(value, 64, 1)
        windows[zero_row] = jnp.zeros(windows.shape[1:], BF16)
        act[zero_row] = jnp.zeros((F, COLS, channels), BF16)
        lane = lax.broadcasted_iota(jnp.int32, (8, LANES), 1)
        col = lax.broadcasted_iota(jnp.int32, (8, LANES), 0)
        low = (lane < 16) | (lane >= 96)
        left_end = (col == 0) & ((lane & 63) < 16)
        right_end = (col == 7) & ((lane & 63) >= 32) & ((lane & 63) < 48)

        def fill(chunk, carry):
            for at in range(4):
                row = chunk * 4 + at
                stack_row = jnp.clip(start - 2 + row, 0, units * owners - 1)
                source = lax.rem(stack_row, owners)
                unit = first_unit(start, 2, source, owners, units, capacity)
                slot = jnp.clip(lax.div(stack_row, owners) - unit, 0, capacity - 1)
                base = source * per_source + slot * 12
                at_low, at_high = {}, {}
                for frame in range(CT + F):
                    for half in range(2):
                        at_row = pl.ds(base + half * (CT + F) + frame, 1)
                        for rolled, into in enumerate((at_low, at_high)):
                            value = jnp.broadcast_to(xs[rolled, at_row, :], (8, LANES))
                            into[half, frame] = pltpu.roll(value, 0, 1, stride=16, stride_axis=0)
                for frame in range(F):
                    pair = [
                        jnp.where(low, at_low[half, frame], at_high[half, frame + 1])
                        for half in range(2)
                    ]
                    last = [at_low[half, frame + 2] for half in range(2)]
                    for lanes, (left, right) in enumerate((pair, last)):
                        near = jnp.where(left_end, 0.0, jnp.where(right_end, right, left))
                        far = jnp.where(right_end, 0.0, jnp.where(left_end, left, right))
                        windows[
                            row,
                            frame * COLS : (frame + 1) * COLS,
                            lanes * LANES : (lanes + 1) * LANES,
                        ] = jnp.concatenate([near, far], axis=0).astype(BF16)
            return carry

        lax.fori_loop(0, lax.div(live + 7, 4), fill, 0)
        gain = gain_ref[...]

        def activate(chunk, carry):
            source_rows = [[], [], []]
            for at in range(4):
                row = chunk * 4 + at
                is_first, is_last = clip_edges(row)
                source_rows[0].append(jnp.where(is_first, zero_row, row))
                source_rows[1].append(jnp.minimum(row + 1, ext - 1))
                source_rows[2].append(jnp.where(is_last, zero_row, jnp.minimum(row + 2, ext - 1)))
            slab = jnp.concatenate(
                [
                    jnp.concatenate([windows[at] for at in source_rows[row_tap]], axis=0)
                    for row_tap in range(3)
                ],
                axis=1,
            )
            size = F * COLS
            sums = jnp.dot(slab, table[...], preferred_element_type=F32)
            first[pl.ds(pl.multiple_of(chunk * 4 * size, size), 4 * size), :] = sums
            for at in range(4):
                value = sums[at * size : (at + 1) * size]
                mean_square = jnp.mean(value * value, axis=-1, keepdims=True)
                value = value * lax.rsqrt(mean_square + EPSILON) * gain
                value = value / (1.0 + jnp.exp(-value))
                act[chunk * 4 + at] = value.astype(BF16).reshape(F, COLS, channels)
            return carry

        lax.fori_loop(0, lax.div(live + 5, 4), activate, 0)
        for copy in copies:
            copy.wait()
        early.start()

    @pl.when(step == pl.num_programs(0) - 1)
    def _():
        early.wait()

    begin = step * block

    @pl.when(begin < live)
    def _():
        source_rows = [[], [], []]
        for row in range(block):
            at = jnp.minimum(begin + row, live - 1) + 1
            is_first, is_last = clip_edges(at)
            source_rows[0].append(jnp.where(is_first, zero_row, at - 1))
            source_rows[1].append(at)
            source_rows[2].append(jnp.where(is_last, zero_row, at + 1))

        def slab(frames):
            pieces = []
            for frame, count in frames:
                for row_tap in range(3):
                    parts = [
                        act[at, frame : frame + count].reshape(count * COLS, channels)
                        for at in source_rows[row_tap]
                    ]
                    pieces.append(jnp.concatenate(parts, axis=0))
            return jnp.concatenate(pieces, axis=1)

        def finish(frames, weight_from, frame_from, count):
            sums = jnp.dot(slab(frames), weights[weight_from:, :], preferred_element_type=F32)
            total = shift_columns(sums, channels)
            parts = []
            for row in range(block):
                at = (begin + row + 1) * F * COLS + frame_from * COLS
                into = pl.ds(pl.multiple_of(at, COLS), count * COLS)
                parts.append(first[into, :])
            return total + jnp.concatenate(parts, axis=0)

        taps = 3 * channels
        late = finish([(0, 2), (1, 2), (2, 2)], 0, 2, 2)
        at_row = lax.broadcasted_iota(jnp.int32, late.shape, 0) // (2 * COLS)
        late = jnp.where(at_row < live - begin, late, 0.0)
        out_ref[...] = late.astype(BF16).reshape(block, 2, COLS, channels)
        part_ref[:, 1] = finish([(0, 1), (1, 1)], taps, 1, 1).reshape(block, COLS, channels)
        part_ref[:, 0] = finish([(0, 1)], 2 * taps, 0, 1).reshape(block, COLS, channels)

    @pl.when(begin >= live)
    def _():
        out_ref[...] = jnp.zeros(out_ref.shape, BF16)


def cached_frames(
    bands, cache_ref, part_ref, mid_ref, late_ref, out_ref, weights, cache, sem, cache_sem,
    *, owners, units, capacity, height, block, channels,
):
    del late_ref
    group = lax.axis_index("seq")
    owner = lax.axis_index("dec")
    live = bands[group, owner]
    start = band_start(bands, group, owner, owners)
    step = pl.program_id(0)
    depth = channels // LANES
    slots = owners * capacity
    edge = lax.rem(height - lax.rem(start - 1 + height, height), height)

    @pl.when(step == 0)
    def _():
        load = pltpu.make_async_copy(cache_ref, cache.at[pl.ds(0, slots)], cache_sem)
        load.start()
        load_mid = pltpu.make_async_copy(mid_ref, weights, sem)
        load_mid.start()
        cache[slots] = jnp.zeros(cache.shape[1:], BF16)
        load.wait()
        load_mid.wait()

    begin = step * block

    @pl.when(begin < live)
    def _():
        def slot_of(at):
            row = jnp.clip(start - 1 + at, 0, units * owners - 1)
            source = lax.rem(row, owners)
            unit = first_unit(start, 1, source, owners, units, capacity)
            return source * capacity + jnp.clip(row // owners - unit, 0, capacity - 1)

        source_rows = [[], [], []]
        for row in range(block):
            at = jnp.minimum(begin + row, live - 1) + 1
            is_first = (at == edge) | (at == edge + height)
            is_last = (at == edge - 1) | (at == edge - 1 + height)
            source_rows[0].append(jnp.where(is_first, slots, slot_of(at - 1)))
            source_rows[1].append(slot_of(at))
            source_rows[2].append(jnp.where(is_last, slots, slot_of(at + 1)))

        def slab(frames):
            pieces = []
            for frame in frames:
                for row_tap in range(3):
                    for part in range(depth):
                        from_tile = (frame * depth + part) * COLS
                        parts = [
                            cache[at, from_tile : from_tile + COLS, :]
                            for at in source_rows[row_tap]
                        ]
                        pieces.append(jnp.concatenate(parts, axis=0))
            return jnp.concatenate(pieces, axis=1)

        at_row = lax.broadcasted_iota(jnp.int32, (block * COLS, channels), 0) // COLS
        taps = 3 * channels
        for frame, frames in ((0, (0, 1)), (1, (1,))):
            sums = jnp.dot(
                slab(frames), weights[: len(frames) * taps, :], preferred_element_type=F32
            )
            total = shift_columns(sums, channels) + part_ref[:, frame].reshape(
                block * COLS, channels
            )
            total = jnp.where(at_row < live - begin, total, 0.0)
            out_ref[:, frame] = total.astype(BF16).reshape(block, COLS, channels)

    @pl.when(begin >= live)
    def _():
        out_ref[...] = jnp.zeros(out_ref.shape, BF16)


def params(mebibytes, **extra):
    return pltpu.CompilerParams(vmem_limit_bytes=mebibytes * 1024 * 1024, **extra)


def shards(latents, cache_lat, cache_act, w_in, w_mid, norm_gain, clip_group, band_rows):
    groups = lax.axis_size("seq")
    owners = lax.axis_size("dec")
    clips = latents.shape[1]
    per_owner = latents.shape[2]
    channels = w_mid.shape[2]
    units = groups * per_owner
    height = per_owner * owners
    stack_rows = groups * height
    band_max = 2 * stack_rows // owners
    act_capacity = (band_max + 2 + owners - 1) // owners
    block = 16 if band_max % 16 == 0 else 8
    any_space = pl.BlockSpec(memory_space=pl.ANY)
    in_vmem = pl.BlockSpec(memory_space=pltpu.VMEM)

    def rows_first(array):
        return jnp.transpose(array[0, :, :, 0, :], (1, 0, 2))

    lat, old, act = rows_first(latents), rows_first(cache_lat), rows_first(cache_act)
    tiles = act.shape[2] // LANES
    lat_rows = (per_owner * 12 + 15) // 16 * 16
    packed_lat = pl.pallas_call(
        functools.partial(pack_latents, per_owner=per_owner, clips=clips),
        grid_spec=pltpu.PrefetchScalarGridSpec(
            num_scalar_prefetch=1,
            grid=(),
            in_specs=[in_vmem, in_vmem],
            out_specs=[in_vmem] * clips,
            scratch_shapes=[pltpu.VMEM((clips * lat_rows, LANES), F32)],
        ),
        out_shape=[jax.ShapeDtypeStruct((lat_rows, LANES), BF16)] * clips,
        compiler_params=params(16),
        name="pack_latents",
    )(clip_group, lat, old)

    def trade(parts):
        return [parts[0]] + [
            lax.ppermute(part, "seq", [(i, i ^ other) for i in range(groups)])
            for other, part in enumerate(parts)
            if other
        ]

    per_step = 3
    packed_act = pl.pallas_call(
        functools.partial(pack_caches, per_step=per_step, clips=clips),
        grid_spec=pltpu.PrefetchScalarGridSpec(
            num_scalar_prefetch=1,
            grid=(per_owner // per_step,),
            in_specs=[
                pl.BlockSpec((per_step, clips, act.shape[2]), lambda step, _: (step, 0, 0))
            ],
            out_specs=[pl.BlockSpec((per_step * tiles, LANES), lambda step, _: (step, 0))] * clips,
            scratch_shapes=[pltpu.VMEM((clips * per_step * tiles, LANES), F32)],
        ),
        out_shape=[jax.ShapeDtypeStruct((per_owner * tiles, LANES), BF16)] * clips,
        compiler_params=params(24),
        name="pack_caches",
    )(clip_group, act)

    def exchange(array, axis):
        return lax.all_to_all(array, axis, split_axis=0, concat_axis=0, tiled=True)

    lat_capacity = (band_max + 4 + owners - 1) // owners
    slice_rows = (lat_capacity * 12 + 15) // 16 * 16
    band_lat = pl.pallas_call(
        functools.partial(
            slice_latents, owners=owners, units=units, capacity=lat_capacity, per_owner=per_owner
        ),
        grid_spec=pltpu.PrefetchScalarGridSpec(
            num_scalar_prefetch=1,
            grid=(),
            in_specs=[in_vmem] * clips,
            out_specs=in_vmem,
            scratch_shapes=[pltpu.VMEM((units * 12 + slice_rows, LANES), F32)],
        ),
        out_shape=jax.ShapeDtypeStruct((owners, slice_rows, LANES), BF16),
        compiler_params=params(16),
        name="slice_latents",
    )(band_rows, *trade(packed_lat))
    band_lat = exchange(band_lat, "dec")
    band_act = pl.pallas_call(
        functools.partial(
            slice_caches, owners=owners, units=units, capacity=act_capacity, tiles=tiles
        ),
        grid_spec=pltpu.PrefetchScalarGridSpec(
            num_scalar_prefetch=1,
            grid=(),
            in_specs=[any_space] * clips,
            out_specs=any_space,
            scratch_shapes=[
                pltpu.VMEM((units * tiles, LANES), BF16),
                pltpu.SemaphoreType.DMA((clips,)),
                pltpu.SemaphoreType.DMA((owners,)),
            ],
        ),
        out_shape=jax.ShapeDtypeStruct((owners, act_capacity * tiles, LANES), BF16),
        compiler_params=params(16),
        name="slice_caches",
    )(band_rows, *trade(packed_act))
    band_lat, band_act = lax.optimization_barrier((band_lat, band_act))
    band_act = exchange(band_act, "dec")

    ext = band_max + 4
    late, part, early_mid = pl.pallas_call(
        functools.partial(
            new_frames, owners=owners, units=units, capacity=lat_capacity, height=height,
            block=block, band_max=band_max, channels=channels,
        ),
        grid_spec=pltpu.PrefetchScalarGridSpec(
            num_scalar_prefetch=1,
            grid=(band_max // block,),
            in_specs=[in_vmem, in_vmem, in_vmem, any_space],
            out_specs=[
                pl.BlockSpec((block, 2, COLS, channels), lambda step, _: (step, 1, 0, 0)),
                pl.BlockSpec((block, 2, COLS, channels), lambda step, _: (step, 0, 0, 0)),
                any_space,
            ],
            scratch_shapes=[
                pltpu.VMEM((9 * channels, 3 * channels), BF16),
                pltpu.VMEM((6 * LANES, channels), BF16),
                pltpu.VMEM((2, owners * slice_rows, LANES), F32),
                pltpu.VMEM((ext + 1, F * COLS, 2 * LANES), BF16),
                pltpu.VMEM(((ext + block) * F * COLS, channels), F32),
                pltpu.VMEM((ext + 1, F, COLS, channels), BF16),
                pltpu.SemaphoreType.DMA((27,)),
                pltpu.SemaphoreType.DMA,
            ],
        ),
        out_shape=[
            jax.ShapeDtypeStruct((band_max, F, COLS, channels), BF16),
            jax.ShapeDtypeStruct((band_max, 2, COLS, channels), F32),
            jax.ShapeDtypeStruct((6 * channels, 3 * channels), BF16),
        ],
        compiler_params=params(50, dimension_semantics=("arbitrary",)),
        cost_estimate=pl.CostEstimate(
            flops=2 * band_max * 9 * COLS * 9 * channels * channels,
            bytes_accessed=16 * 1024 * 1024,
            transcendentals=0,
        ),
        name="new_frames",
    )(band_rows, band_lat, w_in, norm_gain.reshape(1, channels), w_mid)

    slots = owners * act_capacity
    decoded = pl.pallas_call(
        functools.partial(
            cached_frames, owners=owners, units=units, capacity=act_capacity, height=height,
            block=block, channels=channels,
        ),
        grid_spec=pltpu.PrefetchScalarGridSpec(
            num_scalar_prefetch=1,
            grid=(band_max // block,),
            in_specs=[
                any_space,
                pl.BlockSpec((block, 2, COLS, channels), lambda step, _: (step, 0, 0, 0)),
                any_space,
                any_space,
            ],
            out_specs=pl.BlockSpec(
                (block, 2, COLS, channels), lambda step, _: (step, 0, 0, 0)
            ),
            scratch_shapes=[
                pltpu.VMEM((6 * channels, 3 * channels), BF16),
                pltpu.VMEM((slots + 1, tiles, LANES), BF16),
                pltpu.SemaphoreType.DMA,
                pltpu.SemaphoreType.DMA,
            ],
        ),
        out_shape=jax.ShapeDtypeStruct((band_max, F, COLS, channels), BF16),
        input_output_aliases={4: 0},
        compiler_params=params(24, dimension_semantics=("arbitrary",)),
        cost_estimate=pl.CostEstimate(
            flops=2 * band_max * 3 * COLS * 9 * channels * channels,
            bytes_accessed=16 * 1024 * 1024,
            transcendentals=0,
        ),
        name="cached_frames",
    )(band_rows, band_act.reshape(slots, tiles, LANES), part, early_mid, late)
    return decoded.reshape((1, 1) + decoded.shape)


def solution(mesh):
    placed = (
        P("seq", None, None, "dec", None),
        P("seq", None, None, "dec", None),
        P("seq", None, None, "dec", None),
        P(),
        P(),
        P(),
        P(),
        P(),
    )
    return jax.shard_map(
        shards,
        mesh=mesh,
        in_specs=placed,
        out_specs=P("seq", "dec", None, None, None, None),
        check_vma=False,
    )
```

time: 234 us -> 137 us (0.59)
  the two profiles are of different devices: /device:TPU:3 before, /device:TPU:30 now
where the time goes in v2:
time: 137 us; the launch traced here: 135 us
  Pallas kernels  91.2 us (67%)
  starting transfers between devices  17.3 us (13%)
  waiting for transfers between devices  15.5 us (11%)
  local copies, waits for them, and re-layouts  10.5 us (8%)
    pallas_call x1, Pallas kernels, shards(): pl.pallas_call(functools.partial(new_frames, owners=owners, units=units,...  63.4 us
    pallas_call x1, Pallas kernels, shards(): pl.pallas_call(functools.partial(cached_frames, owners=owners, units=unit...  20.6 us
    ppermute x6, waiting for transfers between devices, trade(): lax.ppermute(part, 'seq', [(i, i ^ other) for i in range(groups)])  15.5 us
    unnamed x24, local copies, waits for them, and re-layouts  10.5 us
    all_to_all x2, starting transfers between devices, exchange(): return lax.all_to_all(array, axis, split_axis=0, concat_axis=0, tiled=True)  10.2 us
    ppermute x6, starting transfers between devices, trade(): lax.ppermute(part, 'seq', [(i, i ^ other) for i in range(groups)])  7.11 us
  transfers between devices with their start and end apart: 8, of which 5 were waited for; matrix products, arithmetic and copies ran while one was open for 0% of the time, Pallas kernels for 51%

profile of v2, /device:TPU:30, one launch (start us, length us, event | category | flops | bytes accessed | tf_op | source)
XLA Modules:
  0.0 134.7 jit_solution(18141474915983664005)
XLA Ops:
  0.0 0.9 copy-done.1
  0.9 0.8 copy-done.2
  1.7 0.7 copy-done.3
  2.4 0.7 pack_latents.1
  4.2 2.4 %collective-permute-start.2 = (bf16[144,128]{1,0:T(8,128)(2,1)S(1)}, bf16[144,128]{1,0:T(8,128)(2,1)S(1)}, u32[]{:S(2)}, u32[]{:S(2)}) collective-permute-start(bf16[144,128]{1,0:T(8,128)(2,1)S(1)} %get-tuple-element.21), channel_id=1, source_target_pairs={{0,24},{8,16},{16,8},{24,0},{1,25},{9,17},{17,9},{25,1},{2,26},{10... | collective-permute-start | bytes 110600 | tf_op jit(solution)/shard_map/ppermute | solution.py:420
  7.2 0.6 collective-permute-done.1.refs_2_
  7.8 1.2 collective-permute-done.2.refs_3_
  9.0 0.7 copy-done.5
  9.7 1.8 %slice_latents.1 = bf16[8,160,128]{2,1,0:T(8,128)(2,1)} custom-call(s32[4,8]{1,0:T(4,128)S(1)} %copy-done.5, bf16[144,128]{1,0:T(8,128)(2,1)S(1)} %get-tuple-element.18.refs_0_, bf16[144,128]{1,0:T(8,128)(2,1)S(1)} %collective-permute-done.refs_1_, bf16[144,128]{1,0:T(8,128)(2,1)S(1)} %collective-permute-done.1.refs_2_, ...), custom_call_target="tpu_custom_call" | custom-call | tf_op jit(solution)/shard_map/slice_latents/pallas_call | solution.py:447
  11.5 5.1 %all-to-all-start = ((bf16[8,160,128]{2,1,0:T(8,128)(2,1)}), bf16[8,160,128]{2,1,0:T(8,128)(2,1)S(1)}, u32[]{:S(2)}, u32[]{:S(2)}) async-start(bf16[8,160,128]{2,1,0:T(8,128)(2,1)} %slice_latents.1), calls=%async_computation | async-start | bytes 655360 | tf_op jit(solution)/shard_map/all_to_all | solution.py:443
  16.6 1.3 copy-done
  17.9 0.7 copy-done.4
  18.6 2.2 %pack_caches.1 = (bf16[1152,128]{1,0:T(8,128)(2,1)S(1)}, bf16[1152,128]{1,0:T(8,128)(2,1)S(1)}, bf16[1152,128]{1,0:T(8,128)(2,1)S(1)}, bf16[1152,128]{1,0:T(8,128)(2,1)S(1)}) custom-call(s32[4,4]{1,0:T(4,128)S(1)} %copy-done.4, bf16[12,4,12288]{2,1,0:T(4,128)(2,1)S(1)} %bitcast.12), custom_call_target="tpu_custom_call" | custom-call | tf_op jit(solution)/shard_map/pack_caches/pallas_call | solution.py:426
  20.8 1.6 %collective-permute-start.3 = (bf16[1152,128]{1,0:T(8,128)(2,1)S(1)}, bf16[1152,128]{1,0:T(8,128)(2,1)S(1)}, u32[]{:S(2)}, u32[]{:S(2)}) collective-permute-start(bf16[1152,128]{1,0:T(8,128)(2,1)S(1)} %get-tuple-element.23), channel_id=1, source_target_pairs={{0,8},{8,0},{16,24},{24,16},{1,9},{9,1},{17,25},{25,17},{2,10},{10... | collective-permute-start | bytes 884744 | tf_op jit(solution)/shard_map/ppermute | solution.py:420
  22.4 1.5 %collective-permute-start.4 = (bf16[1152,128]{1,0:T(8,128)(2,1)S(1)}, bf16[1152,128]{1,0:T(8,128)(2,1)S(1)}, u32[]{:S(2)}, u32[]{:S(2)}) collective-permute-start(bf16[1152,128]{1,0:T(8,128)(2,1)S(1)} %get-tuple-element.24), channel_id=1, source_target_pairs={{0,16},{8,24},{16,0},{24,8},{1,17},{9,25},{17,1},{25,9},{2,18},{10... | collective-permute-start | bytes 884744 | tf_op jit(solution)/shard_map/ppermute | solution.py:420
  24.4 6.4 %collective-permute-done.3.refs_1_ = bf16[1152,128]{1,0:T(8,128)(2,1)S(1)} collective-permute-done((bf16[1152,128]{1,0:T(8,128)(2,1)S(1)}, bf16[1152,128]{1,0:T(8,128)(2,1)S(1)}, u32[]{:S(2)}, u32[]{:S(2)}) %collective-permute-start.3) | collective-permute-done | bytes 294944 | tf_op jit(solution)/shard_map/ppermute | solution.py:420
  30.8 6.7 %collective-permute-done.4.refs_2_ = bf16[1152,128]{1,0:T(8,128)(2,1)S(1)} collective-permute-done((bf16[1152,128]{1,0:T(8,128)(2,1)S(1)}, bf16[1152,128]{1,0:T(8,128)(2,1)S(1)}, u32[]{:S(2)}, u32[]{:S(2)}) %collective-permute-start.4) | collective-permute-done | bytes 294944 | tf_op jit(solution)/shard_map/ppermute | solution.py:420
  37.5 0.7 copy-done.6
  38.2 2.4 %slice_caches.1 = bf16[8,1248,128]{2,1,0:T(8,128)(2,1)} custom-call(s32[4,8]{1,0:T(4,128)S(1)} %copy-done.6, bf16[1152,128]{1,0:T(8,128)(2,1)S(1)} %get-tuple-element.22.refs_0_, bf16[1152,128]{1,0:T(8,128)(2,1)S(1)} %collective-permute-done.3.refs_1_, bf16[1152,128]{1,0:T(8,128)(2,1)S(1)} %collective-permute-done.4.refs_2_, ...), custom_call_target="tpu_custom_call" | custom-call | tf_op jit(solution)/shard_map/slice_caches/pallas_call | solution.py:463
  40.6 5.1 %all-to-all-start.1 = ((bf16[8,1248,128]{2,1,0:T(8,128)(2,1)}), bf16[8,1248,128]{2,1,0:T(8,128)(2,1)S(1)}, u32[]{:S(2)}, u32[]{:S(2)}) async-start(bf16[8,1248,128]{2,1,0:T(8,128)(2,1)} %slice_caches.1), calls=%async_computation.1 | async-start | bytes 5111808 | tf_op jit(solution)/shard_map/all_to_all | solution.py:443
  45.8 63.4 %new_frames.1 = (bf16[96,4,16,384]{3,2,1,0:T(8,128)(2,1)}, f32[96,2,16,384]{3,2,1,0:T(8,128)}, bf16[2304,1152]{1,0:T(8,128)(2,1)}) custom-call(s32[4,8]{1,0:T(4,128)S(1)} %copy-done.7, bf16[8,160,128]{2,1,0:T(8,128)(2,1)S(1)} %all-to-all-done.lat_ref, bf16[27,16,384]{2,1,0:T(8,128)(2,1)S(1)} %copy-done.8, f32[1,384]{1,0:T(1,128)S(1)} %reshape.10.gain_ref, ...), custom_call_target="tpu_custom_call" | custom-call | flops 36691771392 | bytes 16777216 | tf_op jit(solution)/shard_map/new_frames/pallas_call | solution.py:486
  109.2 2.5 %copy-done.9 = bf16[2304,1152]{1,0:T(8,128)(2,1)S(1)} copy-done((bf16[2304,1152]{1,0:T(8,128)(2,1)S(1)}, bf16[2304,1152]{1,0:T(8,128)(2,1)}, u32[]{:S(2)}) %copy-start.9) | copy-done | bytes 5308440
  111.7 2.3 %copy-done.10 = f32[96,2,16,384]{3,2,1,0:T(8,128)S(1)} copy-done((f32[96,2,16,384]{3,2,1,0:T(8,128)S(1)}, f32[96,2,16,384]{3,2,1,0:T(8,128)}, u32[]{:S(2)}) %copy-start.10) | copy-done | bytes 4718616
  114.0 20.6 %cached_frames.1 = bf16[96,4,16,384]{3,2,1,0:T(8,128)(2,1)} custom-call(s32[4,8]{1,0:T(4,128)S(1)} %copy-done.7, bf16[104,96,128]{2,1,0:T(8,128)(2,1)S(1)} %bitcast.11, f32[96,2,16,384]{3,2,1,0:T(8,128)S(1)} %copy-done.10, bf16[2304,1152]{1,0:T(8,128)(2,1)S(1)} %copy-done.9, ...), custom_call_target="tpu_custom_call", output_to_operand_aliasing={{}: (4, {})} | custom-call | flops 12230590464 | bytes 16777216 | tf_op jit(solution)/shard_map/cached_frames/pallas_call | solution.py:526
  (23 shorter events, 2.2 us)
Async XLA Ops:
  0.0 0.9 copy-start.1
  0.9 0.8 copy-start.2
  1.7 0.7 copy-start.3
  3.1 4.1 %collective-permute-start = (bf16[144,128]{1,0:T(8,128)(2,1)S(1)}, bf16[144,128]{1,0:T(8,128)(2,1)S(1)}, u32[]{:S(2)}, u32[]{:S(2)}) collective-permute-start(bf16[144,128]{1,0:T(8,128)(2,1)S(1)} %get-tuple-element.19), channel_id=1, source_target_pairs={{0,8},{8,0},{16,24},{24,16},{1,9},{9,1},{17,25},{25,17},{2,10},{10... | collective-permute-start | bytes 110600 | tf_op jit(solution)/shard_map/ppermute | solution.py:420
  3.7 4.2 %collective-permute-start.1 = (bf16[144,128]{1,0:T(8,128)(2,1)S(1)}, bf16[144,128]{1,0:T(8,128)(2,1)S(1)}, u32[]{:S(2)}, u32[]{:S(2)}) collective-permute-start(bf16[144,128]{1,0:T(8,128)(2,1)S(1)} %get-tuple-element.20), channel_id=1, source_target_pairs={{0,16},{8,24},{16,0},{24,8},{1,17},{9,25},{17,1},{25,9},{2,18},{10... | collective-permute-start | bytes 110600 | tf_op jit(solution)/shard_map/ppermute | solution.py:420
  4.2 4.9 %collective-permute-start.2 = (bf16[144,128]{1,0:T(8,128)(2,1)S(1)}, bf16[144,128]{1,0:T(8,128)(2,1)S(1)}, u32[]{:S(2)}, u32[]{:S(2)}) collective-permute-start(bf16[144,128]{1,0:T(8,128)(2,1)S(1)} %get-tuple-element.21), channel_id=1, source_target_pairs={{0,24},{8,16},{16,8},{24,0},{1,25},{9,17},{17,9},{25,1},{2,26},{10... | collective-permute-start | bytes 110600 | tf_op jit(solution)/shard_map/ppermute | solution.py:420
  9.0 0.7 copy-start.5
  11.5 29.1 %all-to-all-start = ((bf16[8,160,128]{2,1,0:T(8,128)(2,1)}), bf16[8,160,128]{2,1,0:T(8,128)(2,1)S(1)}, u32[]{:S(2)}, u32[]{:S(2)}) async-start(bf16[8,160,128]{2,1,0:T(8,128)(2,1)} %slice_latents.1), calls=%async_computation | async-start | bytes 655360 | tf_op jit(solution)/shard_map/all_to_all | solution.py:443
  16.6 1.3 copy-start
  17.9 0.7 copy-start.4
  18.6 27.2 %copy-start.8 = (bf16[27,16,384]{2,1,0:T(8,128)(2,1)S(1)}, bf16[27,16,384]{2,1,0:T(8,128)(2,1)}, u32[]{:S(2)}) copy-start(bf16[27,16,384]{2,1,0:T(8,128)(2,1)} %win_ref.1) | copy-start | bytes 995332
  20.8 24.9 %copy-start.11 = (f32[384]{0:T(512)S(1)}, f32[384]{0:T(512)}, u32[]{:S(2)}) copy-start(f32[384]{0:T(512)} %param.13) | copy-start | bytes 4612
  20.8 24.9 %copy-start.7 = (s32[4,8]{1,0:T(4,128)S(1)}, s32[4,8]{1,0:T(4,128)}, u32[]{:S(2)}) copy-start(s32[4,8]{1,0:T(4,128)} %bands.7) | copy-start | bytes 388
  20.8 9.9 %collective-permute-start.3 = (bf16[1152,128]{1,0:T(8,128)(2,1)S(1)}, bf16[1152,128]{1,0:T(8,128)(2,1)S(1)}, u32[]{:S(2)}, u32[]{:S(2)}) collective-permute-start(bf16[1152,128]{1,0:T(8,128)(2,1)S(1)} %get-tuple-element.23), channel_id=1, source_target_pairs={{0,8},{8,0},{16,24},{24,16},{1,9},{9,1},{17,25},{25,17},{2,10},{10... | collective-permute-start | bytes 884744 | tf_op jit(solution)/shard_map/ppermute | solution.py:420
  22.4 15.1 %collective-permute-start.4 = (bf16[1152,128]{1,0:T(8,128)(2,1)S(1)}, bf16[1152,128]{1,0:T(8,128)(2,1)S(1)}, u32[]{:S(2)}, u32[]{:S(2)}) collective-permute-start(bf16[1152,128]{1,0:T(8,128)(2,1)S(1)} %get-tuple-element.24), channel_id=1, source_target_pairs={{0,16},{8,24},{16,0},{24,8},{1,17},{9,25},{17,1},{25,9},{2,18},{10... | collective-permute-start | bytes 884744 | tf_op jit(solution)/shard_map/ppermute | solution.py:420
  23.9 13.6 %collective-permute-start.5 = (bf16[1152,128]{1,0:T(8,128)(2,1)S(1)}, bf16[1152,128]{1,0:T(8,128)(2,1)S(1)}, u32[]{:S(2)}, u32[]{:S(2)}) collective-permute-start(bf16[1152,128]{1,0:T(8,128)(2,1)S(1)} %get-tuple-element.25), channel_id=1, source_target_pairs={{0,24},{8,16},{16,8},{24,0},{1,25},{9,17},{17,9},{25,1},{2,26},{10... | collective-permute-start | bytes 884744 | tf_op jit(solution)/shard_map/ppermute | solution.py:420
  37.5 0.7 copy-start.6
  40.6 68.6 %all-to-all-start.1 = ((bf16[8,1248,128]{2,1,0:T(8,128)(2,1)}), bf16[8,1248,128]{2,1,0:T(8,128)(2,1)S(1)}, u32[]{:S(2)}, u32[]{:S(2)}) async-start(bf16[8,1248,128]{2,1,0:T(8,128)(2,1)} %slice_caches.1), calls=%async_computation.1 | async-start | bytes 5111808 | tf_op jit(solution)/shard_map/all_to_all | solution.py:443
  109.2 2.5 %copy-start.9 = (bf16[2304,1152]{1,0:T(8,128)(2,1)S(1)}, bf16[2304,1152]{1,0:T(8,128)(2,1)}, u32[]{:S(2)}) copy-start(bf16[2304,1152]{1,0:T(8,128)(2,1)} %get-tuple-element.29.mid_ref) | copy-start | bytes 15925252
  111.7 2.3 %copy-start.10 = (f32[96,2,16,384]{3,2,1,0:T(8,128)S(1)}, f32[96,2,16,384]{3,2,1,0:T(8,128)}, u32[]{:S(2)}) copy-start(f32[96,2,16,384]{3,2,1,0:T(8,128)} %get-tuple-element.28.part_ref) | copy-start | bytes 14155780
